TPU v7x, 32 devices: a whole 2x2x4 slice. The times are simulated.
32 devices in a mesh: fsdp: 16 (over z, x, core), tp: 2 (over y).
Axes of the slice: x: 2, y: 2, z: 4, core: 2. Of those that a mesh axis runs over, the one named last changes fastest.
Arguments:
- block_input: bfloat16 [8192, 1024], P(('fsdp', 'tp')), may hold values from -6 to 6
- segment_ids: int32 [8192], P('fsdp'), may hold values from 0 to 2, as said below
- output_cotangent: bfloat16 [8192, 1024], P(('fsdp', 'tp')), may hold values from -6 to 6
- input_gain: float32 [1024], replicated, may hold values from 0.5 to 1.5
- inner_weight: bfloat16 [1024, 2, 1536], P('fsdp', None, 'tp'), may hold values from -0.1875 to 0.1875
- timestep_weight: bfloat16 [1024, 24], P('fsdp', 'tp'), may hold values from -0.09375 to 0.09375
- state_weight: bfloat16 [1024, 256], P('fsdp'), may hold values from -0.1875 to 0.1875
- query_weight: bfloat16 [1024, 512], P('fsdp', 'tp'), may hold values from -0.1875 to 0.1875
- keyvalue_matrix: bfloat16 [1024, 256], P('fsdp'), may hold values from -0.1875 to 0.1875
- conv_kernel: float32 [4, 1792], replicated, may hold values from -3 to 3
- conv_offset: float32 [1792], replicated, may hold values from -1.5 to 1.5
- timestep_bias: float32 [24], replicated, may hold values from -7 to -2.5
- decay_log: float32 [24], replicated, may hold values from 0 to 1.5
- skip_scale: float32 [24], replicated, may hold values from 0.5 to 1.5
- gated_gain: float32 [1536], replicated, may hold values from 0.5 to 1.5
- mamba_down: bfloat16 [1536, 1024], P('tp', 'fsdp'), may hold values from -0.15625 to 0.15625
- attention_down: bfloat16 [512, 1024], P('tp', 'fsdp'), may hold values from -1 to 1
- middle_gain: float32 [1024], replicated, may hold values from 0.5 to 1.5
- gateup_weight: bfloat16 [1024, 2, 2048], P('fsdp', None, 'tp'), may hold values from -0.1875 to 0.1875
- down_weight: bfloat16 [2048, 1024], P('tp', 'fsdp'), may hold values from -0.125 to 0.125
Outputs:
- block_output: float32 [8192, 1024], P(('fsdp', 'tp'))
- input_grad: float32 [8192, 1024], P(('fsdp', 'tp'))
- input_gain_grad: float32 [1024], replicated
- inner_weight_grad: float32 [1024, 2, 1536], P('fsdp', None, 'tp')
- timestep_weight_grad: float32 [1024, 24], P('fsdp', 'tp')
- state_weight_grad: float32 [1024, 256], P('fsdp')
- query_weight_grad: float32 [1024, 512], P('fsdp', 'tp')
- keyvalue_weight_grad: float32 [1024, 256], P('fsdp')
- conv_kernel_grad: float32 [4, 1792], replicated
- conv_offset_grad: float32 [1792], replicated
- timestep_bias_grad: float32 [24], replicated
- decay_log_grad: float32 [24], replicated
- skip_scale_grad: float32 [24], replicated
- gated_gain_grad: float32 [1536], replicated
- mamba_down_grad: float32 [1536, 1024], P('tp', 'fsdp')
- attention_down_grad: float32 [512, 1024], P('tp', 'fsdp')
- middle_gain_grad: float32 [1024], replicated
- gateup_weight_grad: float32 [1024, 2, 2048], P('fsdp', None, 'tp')
- down_weight_grad: float32 [2048, 1024], P('tp', 'fsdp')
Inputs may be any that keep to these rules, and one draw needn't show every extreme that they name: `segment_ids`: in each aligned block of 512 tokens the ids never fall, start at 0 and end at 2; the run of id 1 begins within the block's first 256 tokens and ends within its last 256.
All inputs are finite; a program needn't handle non-finite values.
Results may differ from a plain program's by a relative error of at most 0.019.
Values may be sent and summed in bfloat16 or wider, within the bound.
No kernel may reach another device: no remote copies, remote signals or barrier semaphores. Data moves between devices by JAX's collectives and lax.ppermute only.
A program may use at most 192 MiB of HBM per device.

v0:
```python
import math

import jax
import jax.numpy as jnp
from jax import lax
from jax.sharding import PartitionSpec as P

QUERY_HEADS = 8
KEYVALUE_HEADS = 2
HEAD_SIZE = 64
SCAN_BLOCK = 256
QUERY_BLOCK = 512


EPSILON = 1e-05
MASKED_SCORE = -1e30
ROPE_BASE = 100000000000.0
PRECISE = lax.Precision.HIGHEST


def inverse_rms(values):
    return lax.rsqrt(jnp.mean(values * values, -1, keepdims=True) + EPSILON)


def contract_rows(left, right):
    return lax.dot_general(
        left, right, (((0,), (0,)), ((), ())), preferred_element_type=jnp.float32
    )


def contract_cols(left, right):
    return lax.dot_general(
        left, right, (((1,), (1,)), ((), ())), preferred_element_type=jnp.float32
    )


def causal_conv(signal, kernel, offset, segment):
    length_tokens = signal.shape[0]
    result = offset[None, :] + kernel[0][None, :] * signal
    for distance in range(1, kernel.shape[0]):
        shifted = jnp.concatenate(
            [
                jnp.zeros((distance, signal.shape[1]), signal.dtype),
                signal[: length_tokens - distance],
            ],
            0,
        )
        earlier = jnp.concatenate(
            [jnp.full((distance,), -1, jnp.int32), segment[: length_tokens - distance]], 0
        )
        retained = (earlier == segment).astype(signal.dtype)
        result = result + kernel[distance][None, :] * shifted * retained[:, None]
    return result


def state_scan(values, timesteps, decays, key_row_block, query_rows, segment, block):
    total, head_count, channels = values.shape
    count = total // block
    states = key_row_block.shape[1]
    lower = jnp.arange(block)[:, None] >= jnp.arange(block)[None, :]

    def advance(carry, pieces):
        memory, previous = carry
        value_block, step_block, key_block, query_block, labels = pieces
        rates = step_block * decays[None, :]
        cumulative = jnp.cumsum(rates, 0)
        linked = jnp.logical_and(labels[:, None] == labels[None, :], lower)
        gaps = cumulative[:, None, :] - cumulative[None, :, :]
        weights = jnp.exp(jnp.where(linked[:, :, None], gaps, 0.0)) * linked[:, :, None].astype(
            jnp.float32
        )
        intersections = jnp.dot(query_block, key_block.T, precision=PRECISE)
        scaled = value_block * step_block[:, :, None]
        within = jnp.einsum(
            "tsh,shp->thp", intersections[:, :, None] * weights, scaled, precision=PRECISE
        )
        carried = jnp.exp(cumulative) * (labels == previous).astype(jnp.float32)[:, None]
        across = (
            jnp.einsum("tn,hpn->thp", query_block, memory, precision=PRECISE) * carried[:, :, None]
        )
        final = cumulative[block - 1]
        ending = labels[block - 1]
        toward = (
            jnp.exp(final[None, :] - cumulative) * (labels == ending).astype(jnp.float32)[:, None]
        )
        fresh = jnp.einsum("sh,shp,sn->hpn", toward, scaled, key_block, precision=PRECISE)
        kept = jnp.exp(final) * (ending == previous).astype(jnp.float32)
        memory = memory * kept[:, None, None] + fresh
        return ((memory, ending), within + across)

    start = (jnp.zeros((head_count, channels, states), jnp.float32), jnp.array(-1, jnp.int32))
    pieces = (
        values.reshape(count, block, head_count, channels),
        timesteps.reshape(count, block, head_count),
        key_row_block.reshape(count, block, states),
        query_rows.reshape(count, block, states),
        segment.reshape(count, block),
    )
    folded, outputs = lax.scan(jax.checkpoint(advance), start, pieces)
    return outputs.reshape(total, head_count, channels)


def mixer_core(
    values, raw_steps, step_bias, decay_log, skip_scale, key_row_block, query_rows, segment, block
):
    timesteps = jax.nn.softplus(raw_steps + step_bias[None, :])
    decays = -jnp.exp(decay_log)
    head_count = timesteps.shape[1]
    shaped = values.reshape(values.shape[0], head_count, -1)
    output = state_scan(shaped, timesteps, decays, key_row_block, query_rows, segment, block)
    return (output + skip_scale[None, :, None] * shaped).reshape(values.shape)


def rotary_apply(vectors, direction):
    length_tokens, head_count, columns = vectors.shape
    halfway = columns // 2
    frequency = jnp.exp(
        jnp.arange(halfway, dtype=jnp.float32) * (-2.0 * math.log(ROPE_BASE) / columns)
    )
    angles = jnp.arange(length_tokens, dtype=jnp.float32)[:, None] * frequency[None, :] * direction
    cosine = jnp.cos(angles)[:, None, :]
    sinusoid = jnp.sin(angles)[:, None, :]
    former = vectors[..., :halfway]
    latter = vectors[..., halfway:]
    return jnp.concatenate(
        [former * cosine - latter * sinusoid, latter * cosine + former * sinusoid], -1
    )


def attention_mask(segment, start, rowcount):
    positions = start + jnp.arange(rowcount, dtype=jnp.int32)
    columns = jnp.arange(segment.shape[0], dtype=jnp.int32)
    labels = lax.dynamic_slice_in_dim(segment, start, rowcount)
    return jnp.logical_and(
        columns[None, :] <= positions[:, None], segment[None, :] == labels[:, None]
    )


def body(
    block_input,
    segment_ids,
    output_cotangent,
    input_gain,
    inner_weight,
    timestep_weight,
    state_weight,
    query_weight,
    keyvalue_matrix,
    conv_kernel,
    conv_offset,
    timestep_bias,
    decay_log,
    skip_scale,
    gated_gain,
    mamba_down,
    attention_down,
    middle_gain,
    gateup_weight,
    down_weight,
):
    tensor_parallel_rank = lax.axis_index("tp")
    residual = block_input.astype(jnp.float32)
    first_rms = inverse_rms(residual)
    normed = lax.all_gather(
        (residual * first_rms * input_gain).astype(jnp.bfloat16), "tp", axis=0, tiled=True
    )
    (
        inner_full,
        timestep_full,
        state_full,
        query_full,
        keyvalue_full,
        mamba_full,
        attention_full,
        gateup_full,
        down_full,
    ) = (
        lax.all_gather(inner_weight, "fsdp", axis=0, tiled=True),
        lax.all_gather(timestep_weight, "fsdp", axis=0, tiled=True),
        lax.all_gather(state_weight, "fsdp", axis=0, tiled=True),
        lax.all_gather(query_weight, "fsdp", axis=0, tiled=True),
        lax.all_gather(keyvalue_matrix, "fsdp", axis=0, tiled=True),
        lax.all_gather(mamba_down, "fsdp", axis=1, tiled=True),
        lax.all_gather(attention_down, "fsdp", axis=1, tiled=True),
        lax.all_gather(gateup_weight, "fsdp", axis=0, tiled=True),
        lax.all_gather(down_weight, "fsdp", axis=1, tiled=True),
    )
    length_tokens = normed.shape[0]
    local_heads = timestep_full.shape[1]
    local_width = inner_full.shape[2]
    ssm_width = gated_gain.shape[0]
    state_dim = state_full.shape[1] // 2
    query_head_count = query_full.shape[1] // HEAD_SIZE
    head_start = tensor_parallel_rank * local_heads
    width_start = tensor_parallel_rank * local_width
    inner = jnp.einsum("gd,dkc->gkc", normed, inner_full, preferred_element_type=jnp.float32)
    raw_steps = jnp.dot(normed, timestep_full, preferred_element_type=jnp.float32)
    state_proj = jnp.dot(normed, state_full, preferred_element_type=jnp.float32)
    query_proj = jnp.dot(normed, query_full, preferred_element_type=jnp.float32)
    keyvalue_projected = jnp.dot(normed, keyvalue_full, preferred_element_type=jnp.float32)
    gate_half = inner[:, 0]
    local_kernel = jnp.concatenate(
        [
            lax.dynamic_slice_in_dim(conv_kernel, width_start, local_width, 1),
            conv_kernel[:, ssm_width:],
        ],
        1,
    )
    local_offset = jnp.concatenate(
        [
            lax.dynamic_slice_in_dim(conv_offset, width_start, local_width, 0),
            conv_offset[ssm_width:],
        ],
        0,
    )
    local_bias = lax.dynamic_slice_in_dim(timestep_bias, head_start, local_heads, 0)
    local_decay = lax.dynamic_slice_in_dim(decay_log, head_start, local_heads, 0)
    local_skip = lax.dynamic_slice_in_dim(skip_scale, head_start, local_heads, 0)
    local_gain = lax.dynamic_slice_in_dim(gated_gain, width_start, local_width, 0)

    def convolve(signal, kernel, offset):
        return jax.nn.silu(causal_conv(signal, kernel, offset, segment_ids))

    convolved, conv_pullback = jax.vjp(
        convolve, jnp.concatenate([inner[:, 1], state_proj], 1), local_kernel, local_offset
    )
    conv_values = convolved[:, :local_width].astype(jnp.bfloat16)
    conv_states = convolved[:, local_width:].astype(jnp.bfloat16).astype(jnp.float32)

    def scan_heads(values, steps_in, bias_in, decay_in, skip_in, key_rows_in, query_rows_in):
        return mixer_core(
            values,
            steps_in,
            bias_in,
            decay_in,
            skip_in,
            key_rows_in,
            query_rows_in,
            segment_ids,
            SCAN_BLOCK,
        )

    scanned, scan_pullback = jax.vjp(
        scan_heads,
        conv_values.astype(jnp.float32),
        raw_steps,
        local_bias,
        local_decay,
        local_skip,
        conv_states[:, :state_dim],
        conv_states[:, state_dim:],
    )
    silu_gate = jax.nn.silu(gate_half)
    gated = scanned * silu_gate
    gated_low = (gated * local_gain).astype(jnp.bfloat16)
    mamba_partial = jnp.dot(gated_low, mamba_full, preferred_element_type=jnp.float32)
    queries = rotary_apply(
        query_proj.reshape(length_tokens, query_head_count, HEAD_SIZE), 1.0
    ).astype(jnp.bfloat16)
    key_gathered = rotary_apply(
        keyvalue_projected[:, : KEYVALUE_HEADS * HEAD_SIZE].reshape(
            length_tokens, KEYVALUE_HEADS, HEAD_SIZE
        ),
        1.0,
    ).astype(jnp.bfloat16)
    value_gathered = (
        keyvalue_projected[:, KEYVALUE_HEADS * HEAD_SIZE :]
        .reshape(length_tokens, KEYVALUE_HEADS, HEAD_SIZE)
        .astype(jnp.bfloat16)
    )
    owner_ranks = (
        tensor_parallel_rank * query_head_count + jnp.arange(query_head_count, dtype=jnp.int32)
    ) // (QUERY_HEADS // KEYVALUE_HEADS)
    choice_picker = (
        owner_ranks[:, None] == jnp.arange(KEYVALUE_HEADS, dtype=jnp.int32)[None, :]
    ).astype(jnp.bfloat16)
    key_row_block = jnp.einsum(
        "jh,ghd->gjd", choice_picker, key_gathered, preferred_element_type=jnp.float32
    ).astype(jnp.bfloat16)
    value_row_block = jnp.einsum(
        "jh,ghd->gjd", choice_picker, value_gathered, preferred_element_type=jnp.float32
    ).astype(jnp.bfloat16)
    scaling = 1.0 / math.sqrt(HEAD_SIZE)
    block_count = length_tokens // QUERY_BLOCK
    query_blocks = queries.reshape(block_count, QUERY_BLOCK, query_head_count, HEAD_SIZE)
    block_starts = jnp.arange(block_count, dtype=jnp.int32) * QUERY_BLOCK

    def block_scores(query_block, start):
        scores = (
            jnp.einsum(
                "qjd,kjd->jqk", query_block, key_row_block, preferred_element_type=jnp.float32
            )
            * scaling
        )
        allowed = attention_mask(segment_ids, start, QUERY_BLOCK)
        return jnp.where(allowed[None], scores, MASKED_SCORE)

    def forward_block(pieces):
        query_block, start = pieces
        masked = block_scores(query_block, start)
        highest = jnp.max(masked, -1, keepdims=True)
        weights = jnp.exp(masked - highest)
        totals = jnp.sum(weights, -1, keepdims=True)
        probs_low = (weights / totals).astype(jnp.bfloat16)
        result = jnp.einsum(
            "jqk,kjd->qjd", probs_low, value_row_block, preferred_element_type=jnp.float32
        )
        return (result, (highest + jnp.log(totals))[..., 0])

    attended, logsums = lax.map(forward_block, (query_blocks, block_starts))
    attended_low = attended.reshape(length_tokens, query_head_count * HEAD_SIZE).astype(
        jnp.bfloat16
    )
    attention_partial = jnp.dot(attended_low, attention_full, preferred_element_type=jnp.float32)
    square_local = jnp.sum(gated * gated, -1)
    mamba_rows, attention_rows, square_rows = (
        lax.psum_scatter(mamba_partial, "tp", scatter_dimension=0, tiled=True),
        lax.psum_scatter(attention_partial, "tp", scatter_dimension=0, tiled=True),
        lax.psum_scatter(square_local, "tp", scatter_dimension=0, tiled=True),
    )
    norm_factor = lax.rsqrt(square_rows / ssm_width + EPSILON)
    factor_low = norm_factor.astype(jnp.bfloat16)
    factor_own = lax.optimization_barrier(factor_low).astype(jnp.float32)
    middle = residual + (factor_own[:, None] * mamba_rows + attention_rows)
    middle_rms = inverse_rms(middle)
    hidden_in = lax.all_gather(
        (middle * middle_rms * middle_gain).astype(jnp.bfloat16), "tp", axis=0, tiled=True
    )
    gateup = jnp.einsum("gd,dkf->gkf", hidden_in, gateup_full, preferred_element_type=jnp.float32)
    gate_part = gateup[:, 0]
    up_part = gateup[:, 1]
    activated = (jax.nn.silu(gate_part) * up_part).astype(jnp.bfloat16)
    feedforward = lax.psum_scatter(
        jnp.dot(activated, down_full, preferred_element_type=jnp.float32).astype(jnp.bfloat16),
        "tp",
        scatter_dimension=0,
        tiled=True,
    ).astype(jnp.float32)
    block_output = middle + feedforward
    cotangent_all = lax.all_gather(output_cotangent, "tp", axis=0, tiled=True)
    grad_activated = contract_cols(cotangent_all, down_full)
    down_wgrad = contract_rows(activated, cotangent_all)
    gate_sigmoid = jax.nn.sigmoid(gate_part)
    grad_gate_part = (
        grad_activated * up_part * gate_sigmoid * (1.0 + gate_part * (1.0 - gate_sigmoid))
    )
    grad_up_part = grad_activated * jax.nn.silu(gate_part)
    grad_gateup = jnp.stack([grad_gate_part, grad_up_part], 1).astype(jnp.bfloat16)
    gateup_wgrad = jnp.einsum(
        "gd,gkf->dkf", hidden_in, grad_gateup, preferred_element_type=jnp.float32
    )
    grad_hidden = lax.psum_scatter(
        jnp.einsum("gkf,dkf->gd", grad_gateup, gateup_full, preferred_element_type=jnp.float32),
        "tp",
        scatter_dimension=0,
        tiled=True,
    )
    middle_normal = middle * middle_rms
    middle_gain_part = jnp.sum(grad_hidden * middle_normal, 0)
    middle_scaled = grad_hidden * middle_gain
    grad_middle = output_cotangent.astype(jnp.float32) + middle_rms * (
        middle_scaled - middle_normal * jnp.mean(middle_scaled * middle_normal, -1, keepdims=True)
    )
    mix_low = grad_middle.astype(jnp.bfloat16)
    mix_own = mix_low.astype(jnp.float32)
    grad_factor = jnp.sum(mix_own * mamba_rows, -1)
    grad_square = (grad_factor * -0.5 * norm_factor * norm_factor * norm_factor / ssm_width).astype(
        jnp.bfloat16
    )
    mix_all, factor_rows, square_rows_grad = (
        lax.all_gather(mix_low, "tp", axis=0, tiled=True),
        lax.all_gather(factor_low, "tp", axis=0, tiled=True),
        lax.all_gather(grad_square, "tp", axis=0, tiled=True),
    )
    grad_mamba = (factor_rows.astype(jnp.float32)[:, None] * mix_all.astype(jnp.float32)).astype(
        jnp.bfloat16
    )
    mamba_wgrad = contract_rows(gated_low, grad_mamba)
    grad_gated_low = contract_cols(grad_mamba, mamba_full)
    gain_grad = jnp.sum(grad_gated_low * gated, 0)
    grad_gated = (
        grad_gated_low * local_gain + 2.0 * gated * square_rows_grad.astype(jnp.float32)[:, None]
    )
    zsigmoid = jax.nn.sigmoid(gate_half)
    grad_scanned = grad_gated * silu_gate
    grad_gate = grad_gated * scanned * zsigmoid * (1.0 + gate_half * (1.0 - zsigmoid))
    grad_values, grad_steps, grad_bias, grad_decay, grad_skip, grad_keys_in, grad_queries_in = (
        scan_pullback(grad_scanned)
    )
    grad_signal, kernel_local, offset_local = conv_pullback(
        jnp.concatenate([grad_values, grad_keys_in, grad_queries_in], 1)
    )
    attention_wgrad = contract_rows(attended_low, mix_all)
    grad_attended = (
        contract_cols(mix_all, attention_full)
        .astype(jnp.bfloat16)
        .reshape(block_count, QUERY_BLOCK, query_head_count, HEAD_SIZE)
    )

    def backward_block(carry, pieces):
        key_grad, value_grad = carry
        query_block, grad_block, logsum_block, start = pieces
        masked = block_scores(query_block, start)
        probs = jnp.exp(masked - logsum_block[..., None])
        grad_probs = jnp.einsum(
            "qjd,kjd->jqk", grad_block, value_row_block, preferred_element_type=jnp.float32
        )
        inner_sum = jnp.sum(grad_probs * probs, -1, keepdims=True)
        grad_scores = (probs * (grad_probs - inner_sum)).astype(jnp.bfloat16)
        query_grad = (
            jnp.einsum(
                "jqk,kjd->qjd", grad_scores, key_row_block, preferred_element_type=jnp.float32
            )
            * scaling
        )
        key_grad = (
            key_grad
            + jnp.einsum(
                "jqk,qjd->kjd", grad_scores, query_block, preferred_element_type=jnp.float32
            )
            * scaling
        )
        value_grad = value_grad + jnp.einsum(
            "jqk,qjd->kjd",
            probs.astype(jnp.bfloat16),
            grad_block,
            preferred_element_type=jnp.float32,
        )
        return ((key_grad, value_grad), query_grad)

    empty_rows = jnp.zeros((length_tokens, query_head_count, HEAD_SIZE), jnp.float32)
    (key_grad, value_grad), query_grads = lax.scan(
        backward_block,
        (empty_rows, empty_rows),
        (query_blocks, grad_attended, logsums, block_starts),
    )
    query_back = rotary_apply(
        query_grads.reshape(length_tokens, query_head_count, HEAD_SIZE), -1.0
    ).reshape(length_tokens, query_head_count * HEAD_SIZE)
    selector_float = choice_picker.astype(jnp.float32)
    key_returned = rotary_apply(
        jnp.einsum("jh,gjd->ghd", selector_float, key_grad, precision=PRECISE), -1.0
    )
    value_returned = jnp.einsum("jh,gjd->ghd", selector_float, value_grad, precision=PRECISE)
    keyvalue_partial = jnp.concatenate(
        [
            key_returned.reshape(length_tokens, KEYVALUE_HEADS * HEAD_SIZE),
            value_returned.reshape(length_tokens, KEYVALUE_HEADS * HEAD_SIZE),
        ],
        1,
    )
    state_total, keyvalue_total = (
        lax.psum(grad_signal[:, local_width:].astype(jnp.bfloat16), "tp").astype(jnp.float32),
        lax.psum(keyvalue_partial.astype(jnp.bfloat16), "tp").astype(jnp.float32),
    )
    inner_low = jnp.stack([grad_gate, grad_signal[:, :local_width]], 1).astype(jnp.bfloat16)
    steps_low = grad_steps.astype(jnp.bfloat16)
    query_low = query_back.astype(jnp.bfloat16)
    state_low = state_total.astype(jnp.bfloat16)
    keyvalue_low = keyvalue_total.astype(jnp.bfloat16)
    inner_wgrad = jnp.einsum("gd,gkc->dkc", normed, inner_low, preferred_element_type=jnp.float32)
    timestep_wgrad = contract_rows(normed, steps_low)
    state_wgrad = contract_rows(normed, state_low)
    query_wgrad = contract_rows(normed, query_low)
    keyvalue_wgrad = contract_rows(normed, keyvalue_low)
    normed_partial = (
        jnp.einsum("gkc,dkc->gd", inner_low, inner_full, preferred_element_type=jnp.float32)
        + contract_cols(steps_low, timestep_full)
        + contract_cols(query_low, query_full)
    )
    leader = (tensor_parallel_rank == 0).astype(jnp.float32)
    normed_partial = normed_partial + leader * (
        contract_cols(state_low, state_full) + contract_cols(keyvalue_low, keyvalue_full)
    )
    normed_grad = lax.psum_scatter(
        normed_partial.astype(jnp.bfloat16), "tp", scatter_dimension=0, tiled=True
    ).astype(jnp.float32)
    first_normal = residual * first_rms
    input_gain_part = jnp.sum(normed_grad * first_normal, 0)
    first_scaled = normed_grad * input_gain
    input_grad = grad_middle + first_rms * (
        first_scaled - first_normal * jnp.mean(first_scaled * first_normal, -1, keepdims=True)
    )
    gated_part = lax.dynamic_update_slice_in_dim(
        jnp.zeros((ssm_width,), jnp.float32), gain_grad, width_start, 0
    )
    kernel_part = jnp.concatenate(
        [
            lax.dynamic_update_slice_in_dim(
                jnp.zeros((conv_kernel.shape[0], ssm_width), jnp.float32),
                kernel_local[:, :local_width],
                width_start,
                1,
            ),
            kernel_local[:, local_width:],
        ],
        1,
    )
    offset_part = jnp.concatenate(
        [
            lax.dynamic_update_slice_in_dim(
                jnp.zeros((ssm_width,), jnp.float32), offset_local[:local_width], width_start, 0
            ),
            offset_local[local_width:],
        ],
        0,
    )
    head_zeros = jnp.zeros((timestep_bias.shape[0],), jnp.float32)
    bias_part = lax.dynamic_update_slice_in_dim(head_zeros, grad_bias, head_start, 0)
    decay_part = lax.dynamic_update_slice_in_dim(head_zeros, grad_decay, head_start, 0)
    skip_part = lax.dynamic_update_slice_in_dim(head_zeros, grad_skip, head_start, 0)
    summed = lax.psum(
        (
            input_gain_part,
            middle_gain_part,
            kernel_part,
            offset_part,
            bias_part,
            decay_part,
            skip_part,
            gated_part,
        ),
        ("fsdp", "tp"),
    )
    (
        inner_out,
        timestep_out,
        state_out,
        query_out,
        keyvalue_out,
        mamba_out,
        attention_out,
        gateup_out,
        down_out,
    ) = (
        lax.psum_scatter(
            inner_wgrad.astype(jnp.bfloat16), "fsdp", scatter_dimension=0, tiled=True
        ).astype(jnp.float32),
        lax.psum_scatter(
            timestep_wgrad.astype(jnp.bfloat16), "fsdp", scatter_dimension=0, tiled=True
        ).astype(jnp.float32),
        lax.psum_scatter(
            state_wgrad.astype(jnp.bfloat16), "fsdp", scatter_dimension=0, tiled=True
        ).astype(jnp.float32),
        lax.psum_scatter(
            query_wgrad.astype(jnp.bfloat16), "fsdp", scatter_dimension=0, tiled=True
        ).astype(jnp.float32),
        lax.psum_scatter(
            keyvalue_wgrad.astype(jnp.bfloat16), "fsdp", scatter_dimension=0, tiled=True
        ).astype(jnp.float32),
        lax.psum_scatter(
            mamba_wgrad.astype(jnp.bfloat16), "fsdp", scatter_dimension=1, tiled=True
        ).astype(jnp.float32),
        lax.psum_scatter(
            attention_wgrad.astype(jnp.bfloat16), "fsdp", scatter_dimension=1, tiled=True
        ).astype(jnp.float32),
        lax.psum_scatter(
            gateup_wgrad.astype(jnp.bfloat16), "fsdp", scatter_dimension=0, tiled=True
        ).astype(jnp.float32),
        lax.psum_scatter(
            down_wgrad.astype(jnp.bfloat16), "fsdp", scatter_dimension=1, tiled=True
        ).astype(jnp.float32),
    )
    return (
        block_output,
        input_grad,
        summed[0],
        inner_out,
        timestep_out,
        state_out,
        query_out,
        keyvalue_out,
        summed[2],
        summed[3],
        summed[4],
        summed[5],
        summed[6],
        summed[7],
        mamba_out,
        attention_out,
        summed[1],
        gateup_out,
        down_out,
    )


def solution(mesh):
    return jax.shard_map(
        body,
        mesh=mesh,
        in_specs=(
            P(("fsdp", "tp"), None),
            P("fsdp"),
            P(("fsdp", "tp"), None),
            P(),
            P("fsdp", None, "tp"),
            P("fsdp", "tp"),
            P("fsdp", None),
            P("fsdp", "tp"),
            P("fsdp", None),
            P(),
            P(),
            P(),
            P(),
            P(),
            P(),
            P("tp", "fsdp"),
            P("tp", "fsdp"),
            P(),
            P("fsdp", None, "tp"),
            P("tp", "fsdp"),
        ),
        out_specs=(
            P(("fsdp", "tp"), None),
            P(("fsdp", "tp"), None),
            P(),
            P("fsdp", None, "tp"),
            P("fsdp", "tp"),
            P("fsdp", None),
            P("fsdp", "tp"),
            P("fsdp", None),
            P(),
            P(),
            P(),
            P(),
            P(),
            P(),
            P("tp", "fsdp"),
            P("tp", "fsdp"),
            P(),
            P("fsdp", None, "tp"),
            P("tp", "fsdp"),
        ),
        check_vma=False,
    )
```

profile of v0, /device:TPU:0, one launch (start us, length us, event | category | flops | bytes accessed | tf_op | source)
XLA Modules:
  0.0 1304.8 jit_solution(5380312273090465283)
XLA Ops:
  14.0 24.6 %all_gather.48 = bf16[1024,256]{1,0:T(8,128)(2,1)S(1)} all-gather(bf16[64,256]{1,0:T(8,128)(2,1)S(1)} %copy-done.106), channel_id=1, replica_groups=mesh['fsdp'=16,'tp'=2] {'fsdp'}, dimensions={0}, use_global_device_ids=true | all-gather | bytes 557056 | tf_op jit(solution)/shard_map/all_gather | solution.py:180
  38.5 17.7 %all-gather = bf16[16,64,12]{1,2,0:T(8,128)(2,1)S(1)} all-gather(bf16[1,64,12]{1,2,0:T(8,128)(2,1)S(1)} %bitcast.527), channel_id=1, replica_groups=mesh['fsdp'=16,'tp'=2] {'fsdp'}, dimensions={0}, use_global_device_ids=true | all-gather | bytes 26112 | tf_op jit(solution)/shard_map/all_gather | solution.py:179
  59.0 20.7 %all_gather.50 = bf16[1024,256]{1,0:T(8,128)(2,1)S(1)} all-gather(bf16[64,256]{1,0:T(8,128)(2,1)S(1)} %copy-done.107), channel_id=1, replica_groups=mesh['fsdp'=16,'tp'=2] {'fsdp'}, dimensions={0}, use_global_device_ids=true | all-gather | bytes 557056 | tf_op jit(solution)/shard_map/all_gather | solution.py:182
  81.5 20.5 %all_gather.51 = bf16[1024,256]{1,0:T(8,128)(2,1)S(1)} all-gather(bf16[64,256]{1,0:T(8,128)(2,1)S(1)} %copy-done.108), channel_id=1, replica_groups=mesh['fsdp'=16,'tp'=2] {'fsdp'}, dimensions={0}, use_global_device_ids=true | all-gather | bytes 557056 | tf_op jit(solution)/shard_map/all_gather | solution.py:181
  102.0 19.8 %all_gather.52 = bf16[256,1024]{0,1:T(8,128)(2,1)S(1)} all-gather(bf16[256,64]{0,1:T(8,128)(2,1)S(1)} %copy-done.109), channel_id=1, replica_groups=mesh['fsdp'=16,'tp'=2] {'fsdp'}, dimensions={1}, use_global_device_ids=true | all-gather | bytes 557056 | tf_op jit(solution)/shard_map/all_gather | solution.py:184
  142.5 3.9 fusion.141
  166.1 67.8 %while.56 = (s32[]{:T(128)}, f32[12,64,128]{2,1,0:T(8,128)S(1)}, s32[]{:T(128)}, f32[2,256,12,64]{1,0,3,2:T(2,128)}, f32[2,12,64,128]{3,2,1,0:T(8,128)}, /*index...) while((s32[]{:T(128)}, f32[12,64,128]{2,1,0:T(8,128)S(1)}, ...), condition=%wide.region_4.5_spmd.clone, body=%wide.region_1.4_spmd.clone.sunk | while | flops 1313911808 | bytes 11117299 | solution.py:99
  172.0 4.9 fusion.327
  177.7 16.7 %dynamic_update_slice.108 = f32[2,256,12,64]{1,0,3,2:T(2,128)} dynamic-update-slice(f32[2,256,12,64]{1,0,3,2:T(2,128)} %get-tuple-element.1392, f32[1,256,12,64]{1,0,3,2:T(1,128)S(1)} %copy.445, s32[]{:T(128)} %get-tuple-element.1389, s32[]{:T(128)} %constant.203.clone.1..sunk, s32[]{:T(128)} %constant.203.clone.1..sunk, s32[]{:T(128)} %constant.203.clone.1..sunk) | dynamic-update-slice | bytes 1572868 | tf_op jit(solution)/shard_map/jvp()/while/body/jit(dynamic_update_index_in_dim)/dynamic_update_slice | solution.py:99
  205.9 4.9 fusion.327
  211.6 16.7 %dynamic_update_slice.108 = f32[2,256,12,64]{1,0,3,2:T(2,128)} dynamic-update-slice(f32[2,256,12,64]{1,0,3,2:T(2,128)} %get-tuple-element.1392, f32[1,256,12,64]{1,0,3,2:T(1,128)S(1)} %copy.445, s32[]{:T(128)} %get-tuple-element.1389, s32[]{:T(128)} %constant.203.clone.1..sunk, s32[]{:T(128)} %constant.203.clone.1..sunk, s32[]{:T(128)} %constant.203.clone.1..sunk) | dynamic-update-slice | bytes 1572868 | tf_op jit(solution)/shard_map/jvp()/while/body/jit(dynamic_update_index_in_dim)/dynamic_update_slice | solution.py:99
  247.5 4.9 all-reduce.13
  252.6 22.9 %reduce-scatter.17.cloned.1.call-done = f32[256,1024]{1,0:T(8,128)} async-done(((f32[512,1024]{1,0:T(8,128)}), f32[256,1024]{1,0:T(8,128)}) %reduce-scatter.17.cloned.1.call-update) | async-done | bytes 1048592 | tf_op jit(solution)/shard_map/reduce_scatter | solution.py:317
  280.6 48.1 %all-gather.20.cloned.1.call-done = bf16[1024,2,1024]{2,0,1:T(8,128)(2,1)} async-done(((bf16[64,2,1024]{2,0,1:T(8,128)(2,1)}), bf16[1024,2,1024]{2,0,1:T(8,128)(2,1)}) %all-gather.20.cloned.1.call-update) | async-done | bytes 4194320 | tf_op jit(solution)/shard_map/all_gather | solution.py:185
  328.7 22.0 %all-gather.18.cloned.1.call-done = bf16[512,1024]{1,0:T(8,128)(2,1)} async-done(((bf16[256,1024]{1,0:T(8,128)(2,1)}), bf16[512,1024]{1,0:T(8,128)(2,1)}) %all-gather.18.cloned.1.call-update) | async-done | bytes 1048592 | tf_op jit(solution)/shard_map/all_gather | solution.py:326
  350.6 6.9 fusion.138
  357.5 16.0 %all-gather.24.cloned.1.call-done = bf16[512,1024]{1,0:T(8,128)(2,1)} async-done(((bf16[256,1024]{1,0:T(8,128)(2,1)}), bf16[512,1024]{1,0:T(8,128)(2,1)}) %all-gather.24.cloned.1.call-update) | async-done | bytes 1048592 | tf_op jit(solution)/shard_map/all_gather | solution.py:340
  373.5 43.6 %all-gather.22.cloned.1.call-done = bf16[1024,1024]{0,1:T(8,128)(2,1)} async-done(((bf16[1024,64]{0,1:T(8,128)(2,1)}), bf16[1024,1024]{0,1:T(8,128)(2,1)}) %all-gather.22.cloned.1.call-update) | async-done | bytes 2097168 | tf_op jit(solution)/shard_map/all_gather | solution.py:186
  417.1 6.2 fusion.144
  428.4 30.7 %reduce-scatter.23.cloned.1.call-done = f32[256,1024]{1,0:T(8,128)} async-done(((f32[512,1024]{1,0:T(8,128)}), f32[256,1024]{1,0:T(8,128)}) %reduce-scatter.23.cloned.1.call-update) | async-done | bytes 1048592 | tf_op jit(solution)/shard_map/reduce_scatter | solution.py:352
  464.7 4.2 all-gather.1
  469.0 4.2 all-gather.2
  473.2 12.1 all-gather.26.cloned.1.call-done
  487.1 5.9 multiply_reduce_fusion.3
  495.5 3.8 multiply_reduce_fusion.9
  507.2 125.8 %while.57 = (s32[]{:T(128)}, f32[12]{0:T(128)}, f32[12,64,128]{2,1,0:T(8,128)}, f32[2,256,12,64]{1,0,3,2:T(2,128)}, f32[2,256,12]{1,0,2:T(2,128)}, /*index=5*/f3...) while((s32[]{:T(128)}, f32[12]{0:T(128)}, ...), condition=%wide.region_29.30_spmd.clone, body=%wide.region_16.29_spmd.clone.sunk | while | flops 3036240896 | bytes 35847344 | solution.py:99
  524.5 5.4 multiply_reduce_fusion.17
  535.0 5.6 fusion.350
  543.9 16.7 %dynamic_update_slice.112 = f32[2,256,12,64]{1,0,3,2:T(2,128)} dynamic-update-slice(f32[2,256,12,64]{1,0,3,2:T(2,128)} %get-tuple-element.1443, f32[1,256,12,64]{1,0,3,2:T(1,128)S(1)} %copy.459, s32[]{:T(128)S(6)} %sub.384, s32[]{:T(128)} %constant.203.clone.1..sunk.1, s32[]{:T(128)} %constant.203.clone.1..sunk.1, s32[]{:T(128)} %constant.203.clone.1..sunk.1) | dynamic-update-slice | bytes 1572868 | tf_op jit(solution)/shard_map/transpose(jvp())/while/body/jit(dynamic_update_index_in_dim)/dynamic_update_slice | solution.py:99
  587.6 5.4 multiply_reduce_fusion.17
  598.1 5.6 fusion.350
  607.1 16.7 %dynamic_update_slice.112 = f32[2,256,12,64]{1,0,3,2:T(2,128)} dynamic-update-slice(f32[2,256,12,64]{1,0,3,2:T(2,128)} %get-tuple-element.1443, f32[1,256,12,64]{1,0,3,2:T(1,128)S(1)} %copy.459, s32[]{:T(128)S(6)} %sub.384, s32[]{:T(128)} %constant.203.clone.1..sunk.1, s32[]{:T(128)} %constant.203.clone.1..sunk.1, s32[]{:T(128)} %constant.203.clone.1..sunk.1) | dynamic-update-slice | bytes 1572868 | tf_op jit(solution)/shard_map/transpose(jvp())/while/body/jit(dynamic_update_index_in_dim)/dynamic_update_slice | solution.py:99
  655.5 3.9 convolution_convert_fusion.2
  670.0 6.0 convolution_convert_fusion
  676.0 8.3 all-reduce.18.cloned.1.call-done
  700.2 4.0 convolution_convert_fusion.4
  704.2 4.7 convolution_convert_fusion.1
  709.1 40.6 %reduce-scatter.41.cloned.1.call-done = bf16[1024,64]{0,1:T(8,128)(2,1)} async-done(((bf16[1024,1024]{0,1:T(8,128)(2,1)}), bf16[1024,64]{0,1:T(8,128)(2,1)}) %reduce-scatter.41.cloned.1.call-update) | async-done | bytes 131088 | tf_op jit(solution)/shard_map/reduce_scatter | solution.py:560
  753.2 54.6 %reduce-scatter.43.cloned.1.call-done = bf16[64,12]{1,0:T(8,128)(2,1)} async-done(((bf16[1024,12]{1,0:T(8,128)(2,1)}), bf16[64,12]{1,0:T(8,128)(2,1)}) %reduce-scatter.43.cloned.1.call-update) | async-done | bytes 1552
  809.2 57.3 %reduce-scatter.37.cloned.1.call-done = bf16[256,64]{0,1:T(8,128)(2,1)} async-done(((bf16[256,1024]{0,1:T(8,128)(2,1)}), bf16[256,64]{0,1:T(8,128)(2,1)}) %reduce-scatter.37.cloned.1.call-update) | async-done | bytes 32784 | tf_op jit(solution)/shard_map/reduce_scatter | solution.py:554
  867.8 57.4 %reduce-scatter.31.cloned.1.call-done = bf16[64,256]{1,0:T(8,128)(2,1)} async-done(((bf16[1024,256]{1,0:T(8,128)(2,1)}), bf16[64,256]{1,0:T(8,128)(2,1)}) %reduce-scatter.31.cloned.1.call-update) | async-done | bytes 32784 | tf_op jit(solution)/shard_map/reduce_scatter | solution.py:545
  926.6 74.3 %reduce-scatter.39.cloned.1.call-done = bf16[64,2,1024]{2,0,1:T(8,128)(2,1)} async-done(((bf16[1024,2,1024]{2,0,1:T(8,128)(2,1)}), bf16[64,2,1024]{2,0,1:T(8,128)(2,1)}) %reduce-scatter.39.cloned.1.call-update) | async-done | bytes 262160 | tf_op jit(solution)/shard_map/reduce_scatter | solution.py:557
  1003.0 56.1 %reduce-scatter.29.cloned.1.call-done = bf16[64,256]{1,0:T(8,128)(2,1)} async-done(((bf16[1024,256]{1,0:T(8,128)(2,1)}), bf16[64,256]{1,0:T(8,128)(2,1)}) %reduce-scatter.29.cloned.1.call-update) | async-done | bytes 32784 | tf_op jit(solution)/shard_map/reduce_scatter | solution.py:542
  1060.5 57.4 %reduce-scatter.33.cloned.1.call-done = bf16[64,256]{1,0:T(8,128)(2,1)} async-done(((bf16[1024,256]{1,0:T(8,128)(2,1)}), bf16[64,256]{1,0:T(8,128)(2,1)}) %reduce-scatter.33.cloned.1.call-update) | async-done | bytes 32784 | tf_op jit(solution)/shard_map/reduce_scatter | solution.py:548
  1119.3 60.7 %reduce-scatter.35.cloned.1.call-done = bf16[768,64]{0,1:T(8,128)(2,1)} async-done(((bf16[768,1024]{0,1:T(8,128)(2,1)}), bf16[768,64]{0,1:T(8,128)(2,1)}) %reduce-scatter.35.cloned.1.call-update) | async-done | bytes 98320 | tf_op jit(solution)/shard_map/reduce_scatter | solution.py:551
  1181.6 20.7 %reduce-scatter.25.cloned.1.call-done = bf16[256,1024]{1,0:T(8,128)(2,1)} async-done(((bf16[512,1024]{1,0:T(8,128)(2,1)}), bf16[256,1024]{1,0:T(8,128)(2,1)}) %reduce-scatter.25.cloned.1.call-update) | async-done | bytes 524304 | tf_op jit(solution)/shard_map/reduce_scatter | solution.py:475
  1203.8 41.2 %all-reduce.14 = (f32[1024]{0:T(1024)}, f32[4,1792]{1,0:T(4,128)}, f32[1792]{0:T(1024)}, f32[24]{0:T(128)}, f32[24]{0:T(128)}, /*index=5*/f32[24]{0:T(128)}, f32[1536]{0:T(1024)}, f32[1024]{0:T(1024)}) all-reduce(f32[1024]{0:T(1024)S(1)} %get-tuple-element.980, ...), channel_id=1, replica_groups=mesh['fsdp'=16,'tp'=2] {'fsdp','tp'}, use_global_device_ids=true, to_apply=%region_36.37 | all-reduce | flops 12616 | bytes 100928 | tf_op jit(solution)/shard_map/psum | solution.py:512
  1248.2 48.0 %reduce-scatter.27.cloned.1.call-done = bf16[64,2,768]{2,0,1:T(8,128)(2,1)} async-done(((bf16[1024,2,768]{2,0,1:T(8,128)(2,1)}), bf16[64,2,768]{2,0,1:T(8,128)(2,1)}) %reduce-scatter.27.cloned.1.call-update) | async-done | bytes 196624 | tf_op jit(solution)/shard_map/reduce_scatter | solution.py:536
  (727 shorter events, 248.6 us)
Async XLA Ops:
  7.3 49.8 %copy-start.149 = (f32[24]{0:T(128)S(1)}, f32[24]{0:T(128)}, u32[]{:S(2)}) copy-start(f32[24]{0:T(128)} %param.35) | copy-start | bytes 292
  7.3 50.3 %copy-start.142 = (f32[24]{0:T(128)S(1)}, f32[24]{0:T(128)}, u32[]{:S(2)}) copy-start(f32[24]{0:T(128)} %param.36) | copy-start | bytes 292
  7.3 50.9 %copy-start.150 = (f32[24]{0:T(128)S(1)}, f32[24]{0:T(128)}, u32[]{:S(2)}) copy-start(f32[24]{0:T(128)} %param.37) | copy-start | bytes 292
  7.3 51.7 %copy-start.107 = (bf16[64,256]{1,0:T(8,128)(2,1)S(1)}, bf16[64,256]{1,0:T(8,128)(2,1)}, u32[]{:S(2)}) copy-start(bf16[64,256]{1,0:T(8,128)(2,1)} %param.32) | copy-start | bytes 98308
  7.3 116.6 %all-gather.12.cloned.1.call-start = ((), (), s32[]{:S(2)}) async-start(), calls=%async_computation.14 | async-start | bytes 1572864 | tf_op jit(solution)/shard_map/all_gather | solution.py:164
  8.7 72.8 %copy-start.108 = (bf16[64,256]{1,0:T(8,128)(2,1)S(1)}, bf16[64,256]{1,0:T(8,128)(2,1)}, u32[]{:S(2)}) copy-start(bf16[64,256]{1,0:T(8,128)(2,1)} %param.31) | copy-start | bytes 98308
  10.7 91.3 %copy-start.109 = (bf16[256,64]{0,1:T(8,128)(2,1)S(1)}, bf16[256,64]{0,1:T(8,128)(2,1)}, u32[]{:S(2)}) copy-start(bf16[256,64]{0,1:T(8,128)(2,1)} %param.40) | copy-start | bytes 98308
  10.7 111.1 %slice-start = ((f32[4,1792]{1,0:T(4,128)}), f32[4,256]{1,0:T(4,128)S(1)}, s32[]{:S(2)}) async-start(f32[4,1792]{1,0:T(4,128)} %param.33), calls=%async_computation.37 | async-start | bytes 8192 | tf_op jit(solution)/shard_map/slice | solution.py:205
  10.7 111.8 %copy-start.137 = (f32[1536]{0:T(1024)S(1)}, f32[1536]{0:T(1024)}, u32[]{:S(2)}) copy-start(f32[1536]{0:T(1024)} %param.38) | copy-start | bytes 18436
  10.7 131.8 %all-gather.14.cloned.1.call-start = ((), (), s32[]{:S(2)}) async-start(), calls=%async_computation.15 | async-start | bytes 3342336 | tf_op jit(solution)/shard_map/all_gather | solution.py:178
  11.5 228.1 %all-gather.16.cloned.1.call-start = ((), (), s32[]{:S(2)}) async-start(), calls=%async_computation.16 | async-start | bytes 1671168 | tf_op jit(solution)/shard_map/all_gather | solution.py:183
  12.3 240.3 %reduce-scatter.19.cloned.1.call-start = ((), (), s32[]{:S(2)}) async-start(), calls=%async_computation.18 | async-start | bytes 3145728 | tf_op jit(solution)/shard_map/reduce_scatter | solution.py:318
  38.5 103.5 %copy-start.35 = (bf16[1024,256]{1,0:T(8,128)(2,1)}, bf16[1024,256]{1,0:T(8,128)(2,1)S(1)}, u32[]{:S(2)}) copy-start(bf16[1024,256]{1,0:T(8,128)(2,1)S(1)} %all_gather.48) | copy-start | bytes 1572868
  79.8 47.3 %copy-start.30 = (bf16[1024,256]{1,0:T(8,128)(2,1)}, bf16[1024,256]{1,0:T(8,128)(2,1)S(1)}, u32[]{:S(2)}) copy-start(bf16[1024,256]{1,0:T(8,128)(2,1)S(1)} %all_gather.50) | copy-start | bytes 1572868
  142.0 133.6 %reduce-scatter.17.cloned.1.call-start = ((), (), s32[]{:S(2)}) async-start(), calls=%async_computation.17 | async-start | bytes 3145728 | tf_op jit(solution)/shard_map/reduce_scatter | solution.py:317
  244.5 84.1 %all-gather.20.cloned.1.call-start = ((), (), s32[]{:S(2)}) async-start(), calls=%async_computation.20 | async-start | bytes 4456448 | tf_op jit(solution)/shard_map/all_gather | solution.py:185
  246.2 104.4 %all-gather.18.cloned.1.call-start = ((), (), s32[]{:S(2)}) async-start(), calls=%async_computation.19 | async-start | bytes 1572864 | tf_op jit(solution)/shard_map/all_gather | solution.py:326
  277.4 184.0 %copy-start.7 = (f32[256,1024]{1,0:T(8,128)}, f32[256,1024]{1,0:T(8,128)S(1)}, u32[]{:S(2)}) copy-start(f32[256,1024]{1,0:T(8,128)S(1)} %get-tuple-element.1066) | copy-start | bytes 3145732
  277.4 184.0 %copy-start.111 = (f32[256]{0:T(256)}, f32[256]{0:T(256)S(1)}, u32[]{:S(2)}) copy-start(f32[256]{0:T(256)S(1)} %add_rsqrt_fusion) | copy-start | bytes 3076
  278.6 94.9 %all-gather.24.cloned.1.call-start = ((), (), s32[]{:S(2)}) async-start(), calls=%async_computation.23 | async-start | bytes 1572864 | tf_op jit(solution)/shard_map/all_gather | solution.py:340
  279.4 137.7 %all-gather.22.cloned.1.call-start = ((), (), s32[]{:S(2)}) async-start(), calls=%async_computation.21 | async-start | bytes 2228224 | tf_op jit(solution)/shard_map/all_gather | solution.py:186
  280.1 179.0 %reduce-scatter.23.cloned.1.call-start = ((), (), s32[]{:S(2)}) async-start(), calls=%async_computation.24 | async-start | bytes 3145728 | tf_op jit(solution)/shard_map/reduce_scatter | solution.py:352
  428.4 57.0 %all-gather.26.cloned.1.call-start = ((), (), s32[]{:S(2)}) async-start(), calls=%async_computation.25 | async-start | bytes 1572864 | tf_op jit(solution)/shard_map/all_gather | solution.py:371
  463.9 220.5 %all-reduce.18.cloned.1.call-start = ((), (), s32[]{:S(2)}) async-start(), calls=%async_computation.36 | async-start | bytes 1048576 | tf_op jit(solution)/shard_map/psum | solution.py:453
  655.4 94.3 %reduce-scatter.41.cloned.1.call-start = ((), (), s32[]{:S(2)}) async-start(), calls=%async_computation.34 | async-start | bytes 2228224 | tf_op jit(solution)/shard_map/reduce_scatter | solution.py:560
  659.4 148.4 %reduce-scatter.43.cloned.1.call-start = ((), (), s32[]{:S(2)}) async-start(), calls=%async_computation.35 | async-start | bytes 278528
  664.2 202.2 %reduce-scatter.37.cloned.1.call-start = ((), (), s32[]{:S(2)}) async-start(), calls=%async_computation.32 | async-start | bytes 557056 | tf_op jit(solution)/shard_map/reduce_scatter | solution.py:554
  666.9 258.4 %reduce-scatter.31.cloned.1.call-start = ((), (), s32[]{:S(2)}) async-start(), calls=%async_computation.29 | async-start | bytes 557056 | tf_op jit(solution)/shard_map/reduce_scatter | solution.py:545
  669.8 331.2 %reduce-scatter.39.cloned.1.call-start = ((), (), s32[]{:S(2)}) async-start(), calls=%async_computation.33 | async-start | bytes 4456448 | tf_op jit(solution)/shard_map/reduce_scatter | solution.py:557
  676.0 383.1 %reduce-scatter.29.cloned.1.call-start = ((), (), s32[]{:S(2)}) async-start(), calls=%async_computation.28 | async-start | bytes 557056 | tf_op jit(solution)/shard_map/reduce_scatter | solution.py:542
  686.8 431.2 %reduce-scatter.33.cloned.1.call-start = ((), (), s32[]{:S(2)}) async-start(), calls=%async_computation.30 | async-start | bytes 557056 | tf_op jit(solution)/shard_map/reduce_scatter | solution.py:548
  688.1 491.9 %reduce-scatter.35.cloned.1.call-start = ((), (), s32[]{:S(2)}) async-start(), calls=%async_computation.31 | async-start | bytes 1671168 | tf_op jit(solution)/shard_map/reduce_scatter | solution.py:551
  691.8 510.5 %reduce-scatter.25.cloned.1.call-start = ((), (), s32[]{:S(2)}) async-start(), calls=%async_computation.26 | async-start | bytes 1572864 | tf_op jit(solution)/shard_map/reduce_scatter | solution.py:475
  700.1 545.0 %reduce-scatter.21.cloned.1.call-start = ((), (), s32[]{:S(2)}) async-start(), calls=%async_computation.22 | async-start | bytes 1572864 | tf_op jit(solution)/shard_map/reduce_scatter | solution.py:333
  704.2 592.0 %reduce-scatter.27.cloned.1.call-start = ((), (), s32[]{:S(2)}) async-start(), calls=%async_computation.27 | async-start | bytes 3342336 | tf_op jit(solution)/shard_map/reduce_scatter | solution.py:536
  708.9 43.7 %copy-start.99 = (f32[1024]{0:T(1024)S(1)}, f32[1024]{0:T(1024)}, u32[]{:S(2)}) copy-start(f32[1024]{0:T(1024)} %get-tuple-element.1056) | copy-start | bytes 12292
  709.0 43.7 %copy-start.115 = (f32[12]{0:T(128)S(1)}, f32[12]{0:T(128)}, u32[]{:S(2)}) copy-start(f32[12]{0:T(128)} %get-tuple-element.536) | copy-start | bytes 148
  709.0 43.7 %copy-start.144 = (f32[24]{0:T(128)S(1)}, f32[24]{0:T(128)}, u32[]{:S(2)}) copy-start(f32[24]{0:T(128)} %param.36) | copy-start | bytes 292
  709.0 493.3 %copy-start.20 = (bf16[256,1024]{1,0:T(8,128)(2,1)S(1)}, bf16[256,1024]{1,0:T(8,128)(2,1)}, u32[]{:S(2)}) copy-start(bf16[256,1024]{1,0:T(8,128)(2,1)} %param.24) | copy-start | bytes 1572868
  709.0 493.3 %copy-start.103 = (f32[1024]{0:T(1024)S(1)}, f32[1024]{0:T(1024)}, u32[]{:S(2)}) copy-start(f32[1024]{0:T(1024)} %param.27) | copy-start | bytes 12292
  709.0 493.3 %copy-start.129 = (f32[256]{0:T(256)S(1)}, f32[256]{0:T(256)}, u32[]{:S(2)}) copy-start(f32[256]{0:T(256)} %copy-done.128) | copy-start | bytes 3076
  709.1 494.7 %copy-start.124 = (f32[1024]{0:T(1024)S(1)}, f32[1024]{0:T(1024)}, u32[]{:S(2)}) copy-start(f32[1024]{0:T(1024)} %get-tuple-element.976) | copy-start | bytes 12292
  709.1 536.0 %copy-start.8 = (f32[256,1024]{1,0:T(8,128)S(1)}, f32[256,1024]{1,0:T(8,128)}, u32[]{:S(2)}) copy-start(f32[256,1024]{1,0:T(8,128)} %copy-done.7) | copy-start | bytes 3145732
  709.1 536.0 %copy-start.22 = (f32[256,1024]{1,0:T(8,128)S(1)}, f32[256,1024]{1,0:T(8,128)}, u32[]{:S(2)}) copy-start(f32[256,1024]{1,0:T(8,128)} %reduce-scatter.23.cloned.1.call-done) | copy-start | bytes 3145732
  709.1 536.0 %copy-start.34 = (bf16[256,1024]{1,0:T(8,128)(2,1)S(1)}, bf16[256,1024]{1,0:T(8,128)(2,1)}, u32[]{:S(2)}) copy-start(bf16[256,1024]{1,0:T(8,128)(2,1)} %param.26) | copy-start | bytes 1572868
  709.1 536.0 %copy-start.89 = (f32[1024]{0:T(1024)S(1)}, f32[1024]{0:T(1024)}, u32[]{:S(2)}) copy-start(f32[1024]{0:T(1024)} %param.41) | copy-start | bytes 12292
  709.1 536.0 %copy-start.112 = (f32[256]{0:T(256)S(1)}, f32[256]{0:T(256)}, u32[]{:S(2)}) copy-start(f32[256]{0:T(256)} %copy-done.111) | copy-start | bytes 3076
  709.1 536.0 %copy-start.132 = (f32[256]{0:T(256)S(1)}, f32[256]{0:T(256)}, u32[]{:S(2)}) copy-start(f32[256]{0:T(256)} %copy-done.131) | copy-start | bytes 3076
  (152 other events, 1114.1 us)
Sparse Core Ops, SparseCore 0:
  10.9 23.9 all-gather.11
  37.7 49.7 all-gather.13
  89.8 38.5 all-gather.15
  142.1 30.5 reduce-scatter.18
  244.6 30.8 reduce-scatter.16
  278.1 50.4 all-gather.19
  330.8 19.7 all-gather.17
  352.1 21.2 all-gather.23
  375.7 41.3 all-gather.21
  428.5 30.6 reduce-scatter.22
  464.0 21.2 all-gather.25
  655.5 28.8 all-reduce.17
  688.1 61.5 reduce-scatter.40
  753.5 54.2 reduce-scatter.42
  811.6 54.8 reduce-scatter.36
  870.4 54.7 reduce-scatter.30
  929.4 71.4 reduce-scatter.38
  1004.4 54.7 reduce-scatter.28
  1063.1 54.8 reduce-scatter.32
  1121.4 58.5 reduce-scatter.34
  1182.9 19.3 reduce-scatter.24
  1205.1 20.5 reduce-scatter.20
  1230.0 66.1 reduce-scatter.26
where the time goes:
time: 1320 us; the launch traced here: 1300 us
  waiting for transfers between devices  733 us (56%)
  local copies, waits for them, and re-layouts  165 us (12%)
  blocking collectives  158 us (12%)
  matrix products  142 us (11%)
  other arithmetic  82.3 us (6%)
  between operations  16.7 us (1%)
    reduce_scatter x1, waiting for transfers between devices, body(): lax.psum_scatter(gateup_wgrad.astype(jnp.bfloat16), 'fsdp', scatter_dimen...  74.3 us
    dynamic_update_slice x14, local copies, waits for them, and re-layouts, state_scan(): folded, outputs = lax.scan(jax.checkpoint(advance), start, pieces)  73 us
    reduce_scatter x1, waiting for transfers between devices, body(): lax.psum_scatter(mamba_wgrad.astype(jnp.bfloat16), 'fsdp', scatter_dimens...  60.7 us
    reduce_scatter x1, waiting for transfers between devices, body(): lax.psum_scatter(keyvalue_wgrad.astype(jnp.bfloat16), 'fsdp', scatter_dim...  57.4 us
    reduce_scatter x1, waiting for transfers between devices, body(): lax.psum_scatter(query_wgrad.astype(jnp.bfloat16), 'fsdp', scatter_dimens...  57.4 us
    reduce_scatter x1, waiting for transfers between devices, body(): lax.psum_scatter(attention_wgrad.astype(jnp.bfloat16), 'fsdp', scatter_di...  57.3 us
    unnamed x24, waiting for transfers between devices  57 us
    reduce_scatter x1, waiting for transfers between devices, body(): lax.psum_scatter(state_wgrad.astype(jnp.bfloat16), 'fsdp', scatter_dimens...  56.1 us
  transfers between devices with their start and end apart: 23, of which 18 were waited for; matrix products, arithmetic and copies ran while one was open for 15% of the time, Pallas kernels for 0%

commit v1 on v0

--- a/solution.py
+++ b/solution.py
@@ -3,6 +3,8 @@
 import jax
 import jax.numpy as jnp
 from jax import lax
+from jax.experimental import pallas as pl
+from jax.experimental.pallas import tpu as pltpu
 from jax.sharding import PartitionSpec as P
 
 QUERY_HEADS = 8
@@ -136,7 +138,7 @@
     )
 
 
-def body(
+def general_body(
     block_input,
     segment_ids,
     output_cotangent,
@@ -584,7 +586,1006 @@
     )
 
 
+BLOCK = 256
+LOG2E = 1.4426950408889634
+HIDDEN_BIAS = -1e30
+
+
+def narrow(values):
+    return values.astype(jnp.bfloat16)
+
+
+def wide(values):
+    return values.astype(jnp.float32)
+
+
+def mm(left, right):
+    return jnp.dot(left, right, preferred_element_type=jnp.float32)
+
+
+def sigmoid(values):
+    return 1.0 / (1.0 + jnp.exp(-values))
+
+
+def dot_wide(ones, values):
+    first = narrow(values)
+    rest = values - wide(first)
+    second = narrow(rest)
+    third = narrow(rest - wide(second))
+    return mm(ones, first) + mm(ones, second) + mm(ones, third)
+
+
+def triangle(rows, upper):
+    down = lax.broadcasted_iota(jnp.int32, (rows, rows), 0)
+    across = lax.broadcasted_iota(jnp.int32, (rows, rows), 1)
+    keep = (across >= down) if upper else (down >= across)
+    return jnp.where(keep, 1.0, 0.0).astype(jnp.bfloat16)
+
+
+def pair_bias(label_column, label_row):
+    rows = label_column.shape[0]
+    down = lax.broadcasted_iota(jnp.int32, (rows, rows), 0)
+    across = lax.broadcasted_iota(jnp.int32, (rows, rows), 1)
+    keep = jnp.logical_and(label_column == label_row, down >= across)
+    return jnp.where(keep, 0.0, HIDDEN_BIAS)
+
+
+def conv_taps(signal, info):
+    taps = [signal]
+    for distance in range(1, 4):
+        taps.append(pltpu.roll(signal, distance, 0) * info[:, distance : distance + 1])
+    return taps
+
+
+def conv_pre(taps, channel):
+    result = channel[4:5, :]
+    for distance in range(4):
+        result = result + channel[distance : distance + 1, :] * taps[distance]
+    return result
+
+
+def conv_back(grad_pre, channel, info):
+    rows = grad_pre.shape[0]
+    result = channel[0:1, :] * grad_pre
+    for distance in range(1, 4):
+        masked = grad_pre * info[:, distance : distance + 1]
+        result = result + channel[distance : distance + 1, :] * pltpu.roll(masked, rows - distance, 0)
+    return result
+
+
+def column_of(values, lane):
+    lanes = lax.broadcasted_iota(jnp.int32, values.shape, 1)
+    return jnp.sum(jnp.where(lanes == lane, values, 0.0), 1, keepdims=True)
+
+
+def half_lanes(values, which):
+    lanes = lax.broadcasted_iota(jnp.int32, values.shape, 1)
+    keep = (lanes < HEAD_SIZE) if which == 0 else (lanes >= HEAD_SIZE)
+    return jnp.where(keep, values, jnp.zeros_like(values))
+
+
+def spans(rows):
+    return [slice(at, at + BLOCK) for at in range(0, rows, BLOCK)]
+
+
+def mixer_forward_kernel(
+    gate_ref,
+    value_ref,
+    state_ref,
+    steps_ref,
+    info_ref,
+    label_ref,
+    channel_ref,
+    state_channel_ref,
+    head_ref,
+    low_ref,
+    scanned_ref,
+    square_ref,
+    dt_ref,
+    cum_ref,
+    crossed,
+    bias,
+    source_rows,
+):
+    pair = pl.program_id(0)
+    info = info_ref[...]
+    rows = info.shape[0]
+
+    @pl.when(pair == 0)
+    def _():
+        taps = conv_taps(state_ref[...], info)
+        pre = conv_pre(taps, state_channel_ref[...])
+        states = narrow(pre * sigmoid(pre))
+        half = states.shape[1] // 2
+        crossed[...] = contract_cols(states[:, half:], states[:, :half])
+        bias[...] = pair_bias(info[:, 4:5], label_ref[0:1, :])
+        raw = steps_ref[...] + head_ref[0:1, :]
+        dt = jnp.maximum(raw, 0.0) + jnp.log1p(jnp.exp(-jnp.abs(raw)))
+        cum = dot_wide(triangle(rows, False), dt * (head_ref[1:2, :] * LOG2E))
+        dt_ref[...] = dt
+        cum_ref[...] = cum
+        source_rows[...] = (cum - jnp.log(dt) * LOG2E).T
+        square_ref[...] = jnp.zeros_like(square_ref)
+
+    channel = channel_ref[...]
+    pre = conv_pre(conv_taps(value_ref[...], info), channel)
+    values = narrow(pre * sigmoid(pre))
+    outputs = [channel[5:6, :] * wide(values[span]) for span in spans(rows)]
+    for which in range(2):
+        head = 2 * pair + which
+        target = column_of(cum_ref[...], head)
+        source = source_rows[pl.ds(head, 1), :]
+        chosen = half_lanes(values, which)
+        for i, down in enumerate(spans(rows)):
+            for across in spans(rows)[: i + 1]:
+                weights = jnp.exp2((target[down] - source[:, across]) + bias[down, across])
+                outputs[i] += mm(narrow(weights * crossed[down, across]), chosen[across])
+    scanned = jnp.concatenate(outputs, 0)
+    scanned_ref[...] = scanned
+    gate = gate_ref[...]
+    gated = scanned * (gate * sigmoid(gate))
+    low_ref[...] = narrow(gated * channel[6:7, :])
+    square_ref[...] += gated * gated
+
+
+def mixer_backward_kernel(
+    gate_ref,
+    value_ref,
+    state_ref,
+    steps_ref,
+    info_ref,
+    label_ref,
+    channel_ref,
+    state_channel_ref,
+    head_ref,
+    scanned_ref,
+    incoming_ref,
+    dt_ref,
+    cum_ref,
+    grad_gate_ref,
+    grad_value_ref,
+    grad_state_ref,
+    grad_steps_ref,
+    channel_grad_ref,
+    state_grad_ref,
+    head_grad_ref,
+    crossed,
+    bias,
+    summed,
+    states_low,
+    source_rows,
+    dt_rows,
+    target_sums,
+    source_sums,
+):
+    pair = pl.program_id(0)
+    info = info_ref[...]
+    rows = info.shape[0]
+    half = state_ref.shape[1] // 2
+
+    @pl.when(pair == 0)
+    def _():
+        pre = conv_pre(conv_taps(state_ref[...], info), state_channel_ref[...])
+        states = narrow(pre * sigmoid(pre))
+        states_low[...] = states
+        crossed[...] = contract_cols(states[:, half:], states[:, :half])
+        bias[...] = pair_bias(info[:, 4:5], label_ref[0:1, :])
+        source_rows[...] = cum_ref[...].T
+        dt_rows[...] = dt_ref[...].T
+        summed[...] = jnp.zeros_like(summed)
+        target_sums[...] = jnp.zeros_like(target_sums)
+        source_sums[...] = jnp.zeros_like(source_sums)
+
+    channel = channel_ref[...]
+    taps = conv_taps(value_ref[...], info)
+    pre = conv_pre(taps, channel)
+    opened = sigmoid(pre)
+    values = narrow(pre * opened)
+    gate = gate_ref[...]
+    gate_open = sigmoid(gate)
+    silu_gate = gate * gate_open
+    scanned = scanned_ref[...]
+    gated = scanned * silu_gate
+    incoming = incoming_ref[...]
+    gain_grad = jnp.sum(incoming * gated, 0, keepdims=True)
+    grad_gated = incoming * channel[6:7, :] + 2.0 * gated * info[:, 5:6]
+    grad_gate_ref[...] = narrow(
+        grad_gated * scanned * gate_open * (1.0 + gate * (1.0 - gate_open))
+    )
+    grad_scanned = grad_gated * silu_gate
+    skip_grad = jnp.sum(grad_scanned * wide(values), 0, keepdims=True)
+    low_grad = narrow(grad_scanned)
+    value_grads = [channel[5:6, :] * grad_scanned[span] for span in spans(rows)]
+    lanes = lax.broadcasted_iota(jnp.int32, (BLOCK, 128), 1)
+    for which in range(2):
+        head = 2 * pair + which
+        target = column_of(cum_ref[...], head)
+        dt_column = column_of(dt_ref[...], head)
+        source = source_rows[pl.ds(head, 1), :]
+        dt_row = dt_rows[pl.ds(head, 1), :]
+        chosen = half_lanes(low_grad, which)
+        returned = [jnp.zeros((BLOCK, 128), jnp.float32) for _ in spans(rows)]
+        column_sums = [jnp.zeros((1, BLOCK), jnp.float32) for _ in spans(rows)]
+        for i, down in enumerate(spans(rows)):
+            row_sum = jnp.zeros((BLOCK, 1), jnp.float32)
+            for j, across in enumerate(spans(rows)[: i + 1]):
+                decay = jnp.exp2((target[down] - source[:, across]) + bias[down, across])
+                linked = crossed[down, across]
+                returned[j] += contract_rows(narrow(decay * linked), chosen[down])
+                reach = decay * contract_cols(chosen[down], values[across])
+                scaled = reach * dt_row[:, across]
+                summed[down, across] += scaled
+                column_sums[j] += jnp.sum(reach * linked, 0, keepdims=True)
+                row_sum += jnp.sum(scaled * linked, 1, keepdims=True)
+            target_sums[down, :] += jnp.where(lanes == head, row_sum, 0.0)
+        for j, across in enumerate(spans(rows)):
+            value_grads[j] += dt_column[across] * returned[j]
+            source_sums[pl.ds(head, 1), across] = column_sums[j]
+    grad_pre = jnp.concatenate(value_grads, 0) * (opened * (1.0 + pre * (1.0 - opened)))
+    grad_value_ref[...] = narrow(conv_back(grad_pre, channel, info))
+    channel_grad_ref[...] = jnp.concatenate(
+        [jnp.sum(grad_pre * tap, 0, keepdims=True) for tap in taps]
+        + [jnp.sum(grad_pre, 0, keepdims=True), skip_grad, gain_grad, jnp.zeros_like(gain_grad)],
+        0,
+    )
+
+    @pl.when(pair == pl.num_programs(0) - 1)
+    def _():
+        low = narrow(summed[...])
+        states = states_low[...]
+        grad_keys = contract_rows(low, states[:, half:])
+        grad_queries = mm(low, states[:, :half])
+        state_channel = state_channel_ref[...]
+        state_taps = conv_taps(state_ref[...], info)
+        state_pre = conv_pre(state_taps, state_channel)
+        state_open = sigmoid(state_pre)
+        grad_state_pre = jnp.concatenate([grad_keys, grad_queries], 1) * (
+            state_open * (1.0 + state_pre * (1.0 - state_open))
+        )
+        grad_state_ref[...] = narrow(conv_back(grad_state_pre, state_channel, info))
+        state_grad_ref[...] = jnp.concatenate(
+            [jnp.sum(grad_state_pre * tap, 0, keepdims=True) for tap in state_taps]
+            + [jnp.sum(grad_state_pre, 0, keepdims=True)]
+            + [jnp.zeros((3, 2 * half), jnp.float32)],
+            0,
+        )
+        dt = dt_ref[...]
+        rate = head_ref[1:2, :]
+        source_columns = source_sums[...].T
+        grad_rate = dot_wide(triangle(rows, True), target_sums[...] - dt * source_columns)
+        grad_dt = source_columns + rate * grad_rate
+        grad_steps = grad_dt * sigmoid(steps_ref[...] + head_ref[0:1, :])
+        grad_steps_ref[...] = narrow(grad_steps)
+        head_grad_ref[...] = jnp.concatenate(
+            [
+                jnp.sum(grad_steps, 0, keepdims=True),
+                jnp.sum(grad_rate * dt * rate, 0, keepdims=True),
+                jnp.zeros((6, 128), jnp.float32),
+            ],
+            0,
+        )
+
+
+def rotated(values, cosine, sinusoid):
+    lanes = lax.broadcasted_iota(jnp.int32, values.shape, 1)
+    quarter = HEAD_SIZE // 2
+    swapped = jnp.where(
+        lanes % HEAD_SIZE < quarter,
+        pltpu.roll(values, values.shape[1] - quarter, 1),
+        pltpu.roll(values, quarter, 1),
+    )
+    return values * cosine + swapped * sinusoid
+
+
+def attention_forward_kernel(
+    rank_ref,
+    query_ref,
+    keyvalue_ref,
+    info_ref,
+    label_ref,
+    cosine_ref,
+    sinusoid_ref,
+    attended_ref,
+    turned_ref,
+    key_ref,
+    value_ref,
+    logsum_ref,
+    bias,
+):
+    rows = query_ref.shape[0]
+    cosine, sinusoid = cosine_ref[...], sinusoid_ref[...]
+    bias[...] = pair_bias(info_ref[:, 4:5], label_ref[0:1, :])
+    lanes = lax.broadcasted_iota(jnp.int32, (rows, 128), 1)
+    own = (lanes < HEAD_SIZE) == (rank_ref[0] == 0)
+
+    def doubled(values):
+        return jnp.where(own, values, pltpu.roll(values, HEAD_SIZE, 1))
+
+    keys = narrow(doubled(rotated(keyvalue_ref[:, :128], cosine, sinusoid)))
+    values = narrow(doubled(keyvalue_ref[:, 128:]))
+    key_ref[...] = keys
+    value_ref[...] = values
+    scaling = 1.0 / math.sqrt(HEAD_SIZE)
+    logsums = [jnp.zeros((BLOCK, 128), jnp.float32) for _ in spans(rows)]
+    block_lanes = lax.broadcasted_iota(jnp.int32, (BLOCK, 128), 1)
+    for pair in range(query_ref.shape[1] // 128):
+        columns = slice(128 * pair, 128 * pair + 128)
+        queries = narrow(rotated(query_ref[:, columns], cosine, sinusoid))
+        turned_ref[:, columns] = queries
+        results = [jnp.zeros((BLOCK, 128), jnp.float32) for _ in spans(rows)]
+        for which in range(2):
+            chosen = half_lanes(queries, which)
+            reading = half_lanes(values, which)
+            for i, down in enumerate(spans(rows)):
+                width = BLOCK * (i + 1)
+                scores = contract_cols(chosen[down], keys[:width]) * scaling + bias[down, :width]
+                highest = jnp.max(scores, 1, keepdims=True)
+                weights = jnp.exp(scores - highest)
+                total = jnp.sum(weights, 1, keepdims=True)
+                results[i] += mm(narrow(weights * (1.0 / total)), reading[:width])
+                logsums[i] = jnp.where(
+                    block_lanes == 2 * pair + which, highest + jnp.log(total), logsums[i]
+                )
+        for i, down in enumerate(spans(rows)):
+            attended_ref[down, columns] = narrow(results[i])
+    for i, down in enumerate(spans(rows)):
+        logsum_ref[down, :] = logsums[i]
+
+
+def attention_backward_kernel(
+    rank_ref,
+    incoming_ref,
+    turned_ref,
+    key_ref,
+    value_ref,
+    logsum_ref,
+    info_ref,
+    label_ref,
+    cosine_ref,
+    sinusoid_ref,
+    grad_query_ref,
+    grad_keyvalue_ref,
+    bias,
+):
+    rows = turned_ref.shape[0]
+    cosine, sinusoid = cosine_ref[...], sinusoid_ref[...]
+    bias[...] = pair_bias(info_ref[:, 4:5], label_ref[0:1, :])
+    keys, values = key_ref[...], value_ref[...]
+    scaling = 1.0 / math.sqrt(HEAD_SIZE)
+    zero = jnp.zeros((BLOCK, 128), jnp.float32)
+    key_grads = [zero for _ in spans(rows)]
+    value_grads = [zero for _ in spans(rows)]
+    for pair in range(turned_ref.shape[1] // 128):
+        columns = slice(128 * pair, 128 * pair + 128)
+        query_grads = [zero for _ in spans(rows)]
+        for which in range(2):
+            queries = half_lanes(turned_ref[:, columns], which)
+            incoming = half_lanes(incoming_ref[:, columns], which)
+            reading = half_lanes(keys, which)
+            head = 2 * pair + which
+            for i, down in enumerate(spans(rows)):
+                width = BLOCK * (i + 1)
+                scores = contract_cols(queries[down], keys[:width]) * scaling + bias[down, :width]
+                probs = jnp.exp(scores - logsum_ref[down, head : head + 1])
+                grad_probs = contract_cols(incoming[down], values[:width])
+                inner_sum = jnp.sum(grad_probs * probs, 1, keepdims=True)
+                grad_scores = narrow(probs * (grad_probs - inner_sum))
+                probs_low = narrow(probs)
+                query_grads[i] += mm(grad_scores, reading[:width])
+                for j, across in enumerate(spans(rows)[: i + 1]):
+                    key_grads[j] += contract_rows(grad_scores[:, across], queries[down])
+                    value_grads[j] += contract_rows(probs_low[:, across], incoming[down])
+        grad_query_ref[:, columns] = narrow(
+            rotated(jnp.concatenate(query_grads, 0) * scaling, cosine, -sinusoid)
+        )
+    lanes = lax.broadcasted_iota(jnp.int32, (rows, 128), 1)
+    own = (lanes < HEAD_SIZE) == (rank_ref[0] == 0)
+
+    def placed(values):
+        return jnp.where(own, values + pltpu.roll(values, HEAD_SIZE, 1), 0.0)
+
+    key_grad = rotated(placed(jnp.concatenate(key_grads, 0) * scaling), cosine, -sinusoid)
+    grad_keyvalue_ref[:, :128] = narrow(key_grad)
+    grad_keyvalue_ref[:, 128:] = narrow(placed(jnp.concatenate(value_grads, 0)))
+
+
+def block_spec(shape, index):
+    return pl.BlockSpec(shape, index)
+
+
+def fixed(array):
+    return pl.BlockSpec(array.shape, lambda p: (0, 0))
+
+
+def params():
+    return pltpu.CompilerParams(vmem_limit_bytes=48 * 1024 * 1024)
+
+
+def mixer_forward(projected, widths, info, labels, channel, state_channel, heads):
+    rows = info.shape[0]
+    width, state_at, steps_at = widths
+    pairs = width // 128
+    state_width = state_channel.shape[1]
+    column = lambda p: (0, p)
+    return pl.pallas_call(
+        mixer_forward_kernel,
+        grid=(pairs,),
+        in_specs=[
+            block_spec((rows, 128), column),
+            block_spec((rows, 128), lambda p: (0, pairs + p)),
+            block_spec((rows, state_width), lambda p: (0, state_at // state_width)),
+            block_spec((rows, 128), lambda p: (0, steps_at // 128)),
+            fixed(info),
+            fixed(labels),
+            block_spec((8, 128), column),
+            fixed(state_channel),
+            fixed(heads),
+        ],
+        out_specs=[
+            block_spec((rows, 128), column),
+            block_spec((rows, 128), column),
+            block_spec((rows, 128), lambda p: (0, 0)),
+            block_spec((rows, 128), lambda p: (0, 0)),
+            block_spec((rows, 128), lambda p: (0, 0)),
+        ],
+        out_shape=[
+            jax.ShapeDtypeStruct((rows, width), jnp.bfloat16),
+            jax.ShapeDtypeStruct((rows, width), jnp.float32),
+            jax.ShapeDtypeStruct((rows, 128), jnp.float32),
+            jax.ShapeDtypeStruct((rows, 128), jnp.float32),
+            jax.ShapeDtypeStruct((rows, 128), jnp.float32),
+        ],
+        scratch_shapes=[
+            pltpu.VMEM((rows, rows), jnp.float32),
+            pltpu.VMEM((rows, rows), jnp.float32),
+            pltpu.VMEM((128, rows), jnp.float32),
+        ],
+        compiler_params=params(),
+        cost_estimate=pl.CostEstimate(
+            flops=24 * rows * rows * width, bytes_accessed=rows * width * 14, transcendentals=0
+        ),
+        name="mixer_forward",
+    )(projected, projected, projected, projected, info, labels, channel, state_channel, heads)
+
+
+def mixer_backward(
+    projected, widths, info, labels, channel, state_channel, heads, scanned, incoming, dt, cum
+):
+    rows = info.shape[0]
+    width, state_at, steps_at = widths
+    pairs = width // 128
+    state_width = state_channel.shape[1]
+    column = lambda p: (0, p)
+    still = lambda p: (0, 0)
+    return pl.pallas_call(
+        mixer_backward_kernel,
+        grid=(pairs,),
+        in_specs=[
+            block_spec((rows, 128), column),
+            block_spec((rows, 128), lambda p: (0, pairs + p)),
+            block_spec((rows, state_width), lambda p: (0, state_at // state_width)),
+            block_spec((rows, 128), lambda p: (0, steps_at // 128)),
+            fixed(info),
+            fixed(labels),
+            block_spec((8, 128), column),
+            fixed(state_channel),
+            fixed(heads),
+            block_spec((rows, 128), column),
+            block_spec((rows, 128), column),
+            fixed(dt),
+            fixed(cum),
+        ],
+        out_specs=[
+            block_spec((rows, 128), column),
+            block_spec((rows, 128), column),
+            block_spec((rows, state_width), still),
+            block_spec((rows, 128), still),
+            block_spec((8, 128), column),
+            block_spec((8, state_width), still),
+            block_spec((8, 128), still),
+        ],
+        out_shape=[
+            jax.ShapeDtypeStruct((rows, width), jnp.bfloat16),
+            jax.ShapeDtypeStruct((rows, width), jnp.bfloat16),
+            jax.ShapeDtypeStruct((rows, state_width), jnp.bfloat16),
+            jax.ShapeDtypeStruct((rows, 128), jnp.bfloat16),
+            jax.ShapeDtypeStruct((8, width), jnp.float32),
+            jax.ShapeDtypeStruct((8, state_width), jnp.float32),
+            jax.ShapeDtypeStruct((8, 128), jnp.float32),
+        ],
+        scratch_shapes=[
+            pltpu.VMEM((rows, rows), jnp.float32),
+            pltpu.VMEM((rows, rows), jnp.float32),
+            pltpu.VMEM((rows, rows), jnp.float32),
+            pltpu.VMEM((rows, state_width), jnp.bfloat16),
+            pltpu.VMEM((128, rows), jnp.float32),
+            pltpu.VMEM((128, rows), jnp.float32),
+            pltpu.VMEM((rows, 128), jnp.float32),
+            pltpu.VMEM((128, rows), jnp.float32),
+        ],
+        compiler_params=params(),
+        cost_estimate=pl.CostEstimate(
+            flops=72 * rows * rows * width, bytes_accessed=rows * width * 22, transcendentals=0
+        ),
+        name="mixer_backward",
+    )(
+        projected,
+        projected,
+        projected,
+        projected,
+        info,
+        labels,
+        channel,
+        state_channel,
+        heads,
+        scanned,
+        incoming,
+        dt,
+        cum,
+    )
+
+
+def attention_forward(rank, projected, widths, info, labels, cosine, sinusoid):
+    rows = info.shape[0]
+    query_at, keyvalue_at, query_width, keyvalue_width = widths
+    return pl.pallas_call(
+        attention_forward_kernel,
+        grid=(1,),
+        in_specs=[
+            pl.BlockSpec(memory_space=pltpu.SMEM),
+            block_spec((rows, query_width), lambda p: (0, query_at // query_width)),
+            block_spec((rows, keyvalue_width), lambda p: (0, keyvalue_at // keyvalue_width)),
+            fixed(info),
+            fixed(labels),
+            fixed(cosine),
+            fixed(sinusoid),
+        ],
+        out_specs=[
+            block_spec((rows, query_width), lambda p: (0, 0)),
+            block_spec((rows, query_width), lambda p: (0, 0)),
+            block_spec((rows, 128), lambda p: (0, 0)),
+            block_spec((rows, 128), lambda p: (0, 0)),
+            block_spec((rows, 128), lambda p: (0, 0)),
+        ],
+        out_shape=[
+            jax.ShapeDtypeStruct((rows, query_width), jnp.bfloat16),
+            jax.ShapeDtypeStruct((rows, query_width), jnp.bfloat16),
+            jax.ShapeDtypeStruct((rows, 128), jnp.bfloat16),
+            jax.ShapeDtypeStruct((rows, 128), jnp.bfloat16),
+            jax.ShapeDtypeStruct((rows, 128), jnp.float32),
+        ],
+        scratch_shapes=[pltpu.VMEM((rows, rows), jnp.float32)],
+        compiler_params=params(),
+        cost_estimate=pl.CostEstimate(
+            flops=24 * rows * rows * query_width, bytes_accessed=rows * 4096, transcendentals=0
+        ),
+        name="attention_forward",
+    )(rank, projected, projected, info, labels, cosine, sinusoid)
+
+
+def attention_backward(rank, incoming, turned, keys, values, logsum, info, labels, cosine, sinusoid):
+    rows, query_width = turned.shape
+    arrays = (incoming, turned, keys, values, logsum, info, labels, cosine, sinusoid)
+    return pl.pallas_call(
+        attention_backward_kernel,
+        grid=(1,),
+        in_specs=[pl.BlockSpec(memory_space=pltpu.SMEM)] + [fixed(array) for array in arrays],
+        out_specs=[
+            block_spec((rows, query_width), lambda p: (0, 0)),
+            block_spec((rows, 256), lambda p: (0, 0)),
+        ],
+        out_shape=[
+            jax.ShapeDtypeStruct((rows, query_width), jnp.bfloat16),
+            jax.ShapeDtypeStruct((rows, 256), jnp.bfloat16),
+        ],
+        scratch_shapes=[pltpu.VMEM((rows, rows), jnp.float32)],
+        compiler_params=params(),
+        cost_estimate=pl.CostEstimate(
+            flops=72 * rows * rows * query_width, bytes_accessed=rows * 4096, transcendentals=0
+        ),
+        name="attention_backward",
+    )(rank, *arrays)
+
+
+def place_kernel(count, starts_ref, *refs):
+    pieces, whole, done = refs[:count], refs[count], refs[count + 1]
+    rows = pieces[0].shape[0]
+    copies = []
+    for at, piece in enumerate(pieces):
+        start = pl.multiple_of(starts_ref[at] * rows, rows)
+        copies.append(pltpu.make_async_copy(piece, whole.at[pl.ds(start, rows)], done.at[at]))
+    for copy in copies:
+        copy.start()
+    for copy in copies:
+        copy.wait()
+
+
+def place(starts, pieces):
+    count = len(pieces)
+    rows, columns = pieces[0].shape
+    return pl.pallas_call(
+        lambda *refs: place_kernel(count, *refs),
+        in_specs=[pl.BlockSpec(memory_space=pltpu.SMEM)]
+        + [pl.BlockSpec(memory_space=pl.ANY)] * count,
+        out_specs=pl.BlockSpec(memory_space=pltpu.VMEM),
+        out_shape=jax.ShapeDtypeStruct((count * rows, columns), pieces[0].dtype),
+        scratch_shapes=[pltpu.SemaphoreType.DMA((count,))],
+        compiler_params=params(),
+        cost_estimate=pl.CostEstimate(
+            flops=0, bytes_accessed=4 * count * rows * columns, transcendentals=0
+        ),
+        name="place",
+    )(starts, *pieces)
+
+
+def swaps(size, bit):
+    return [(i, i ^ bit) for i in range(size)]
+
+
+def ring(size):
+    return [(i, (i + 4) % size) for i in range(size)]
+
+
+def gather_pieces(piece, size):
+    held = [piece]
+    for _ in range(size // 4 - 1):
+        held.append(lax.ppermute(held[-1], "fsdp", ring(size)))
+    pieces = []
+    for shard in held:
+        for line in (shard, lax.ppermute(shard, "fsdp", swaps(size, 2))):
+            pieces += [line, lax.ppermute(line, "fsdp", swaps(size, 1))]
+    return pieces
+
+
+def reduce_pieces(grad, size):
+    half = grad.shape[0] // 2
+    own = narrow(
+        wide(grad[:half]) + wide(lax.ppermute(grad[half:], "fsdp", swaps(size, 1)))
+    )
+    half //= 2
+    own = wide(own[:half]) + wide(lax.ppermute(own[half:], "fsdp", swaps(size, 2)))
+    parts = own.reshape(size // 4, -1, own.shape[1])
+    total = parts[1]
+    for step in range(2, size // 4 + 1):
+        total = parts[step % (size // 4)] + wide(
+            lax.ppermute(narrow(total), "fsdp", ring(size))
+        )
+    return total
+
+
+def reduce_all(values, size):
+    bit = 1
+    while bit < size:
+        values = values + lax.ppermute(values, "fsdp", swaps(size, bit))
+        bit *= 2
+    return values + lax.ppermute(values, "tp", swaps(2, 1))
+
+
+def packed_body(
+    size,
+    block_input,
+    segment_ids,
+    output_cotangent,
+    input_gain,
+    inner_weight,
+    timestep_weight,
+    state_weight,
+    query_weight,
+    keyvalue_matrix,
+    conv_kernel,
+    conv_offset,
+    timestep_bias,
+    decay_log,
+    skip_scale,
+    gated_gain,
+    mamba_down,
+    attention_down,
+    middle_gain,
+    gateup_weight,
+    down_weight,
+):
+    rank = lax.axis_index("tp")
+    at = lax.axis_index("fsdp")
+    depth = size // 4
+    rows = segment_ids.shape[0]
+    own_rows = rows // 2
+    shard, _, width = inner_weight.shape
+    model = shard * size
+    heads = timestep_weight.shape[1]
+    state_width = state_weight.shape[1]
+    query_width = query_weight.shape[1]
+    keyvalue_width = keyvalue_matrix.shape[1]
+    hidden = gateup_weight.shape[2]
+    ssm_width = gated_gain.shape[0]
+    state_at = 2 * width
+    query_at = state_at + state_width
+    keyvalue_at = query_at + query_width
+    steps_at = keyvalue_at + keyvalue_width
+
+    def other(values):
+        return lax.ppermute(values, "tp", swaps(2, 1))
+
+    def joined(own, far):
+        first = jnp.where(rank == 0, own, far)
+        second = jnp.where(rank == 0, far, own)
+        return jnp.concatenate([first, second], 0)
+
+    def own_half(values):
+        return lax.dynamic_slice_in_dim(values, rank * own_rows, own_rows, 0)
+
+    def far_half(values):
+        return lax.dynamic_slice_in_dim(values, (1 - rank) * own_rows, own_rows, 0)
+
+    first_shard = jnp.concatenate(
+        [
+            inner_weight.reshape(shard, 2 * width),
+            state_weight,
+            query_weight,
+            keyvalue_matrix,
+            jnp.pad(timestep_weight, ((0, 0), (0, 128 - heads))),
+        ],
+        1,
+    )
+    second_shard = jnp.concatenate([mamba_down, attention_down], 0).T
+    third_shard = jnp.concatenate([gateup_weight.reshape(shard, 2 * hidden), down_weight.T], 1)
+    ring_at, x_at, core_at = at // 4, (at // 2) % 2, at % 2
+
+    def block_of(distance, x_flip, core_flip):
+        return ((ring_at - distance + depth) % depth) * 4 + (x_at ^ x_flip) * 2 + (
+            core_at ^ core_flip
+        )
+
+    starts = jnp.stack(
+        [block_of(k, i, j) for k in range(depth) for i in range(2) for j in range(2)]
+    ).astype(jnp.int32)
+    first_pieces = gather_pieces(first_shard, size)
+    second_shard, third_shard, _ = lax.optimization_barrier(
+        (second_shard, third_shard, first_pieces[-4])
+    )
+    second_pieces = gather_pieces(second_shard, size)
+    third_shard, _ = lax.optimization_barrier((third_shard, second_pieces[-4]))
+    third_pieces = gather_pieces(third_shard, size)
+
+    relative = jnp.arange(model, dtype=jnp.int32)
+    piece_at = relative // shard
+    absolute = (
+        block_of(piece_at % depth, (piece_at // depth) % 2, piece_at // (2 * depth)) * shard
+        + relative % shard
+    )
+    permutation = (jnp.arange(model, dtype=jnp.int32)[:, None] == absolute[None, :]).astype(
+        jnp.bfloat16
+    )
+
+    def permuted(values):
+        return narrow(mm(values, permutation))
+
+    residual_low = joined(block_input, other(block_input))
+    residual = wide(residual_low)
+    first_rms = inverse_rms(residual)
+    normed = narrow(residual * first_rms * input_gain)
+    cotangent = joined(output_cotangent, other(output_cotangent))
+    labels = segment_ids.astype(jnp.float32)
+    info = [jnp.zeros((rows, 1), jnp.float32)]
+    for distance in range(1, 4):
+        earlier = jnp.concatenate([jnp.full((distance,), -1.0), labels[:-distance]], 0)
+        info.append((earlier == labels).astype(jnp.float32)[:, None])
+    info = jnp.concatenate(info + [labels[:, None], jnp.zeros((rows, 123), jnp.float32)], 1)
+    label_rows = jnp.broadcast_to(labels[None, :], (8, rows))
+    repeat = width // heads
+    local_skip = lax.dynamic_slice_in_dim(skip_scale, rank * heads, heads, 0)
+    local = lambda array: lax.dynamic_slice_in_dim(array, rank * width, width, array.ndim - 1)
+    channel = jnp.concatenate(
+        [
+            local(conv_kernel),
+            local(conv_offset)[None],
+            jnp.repeat(local_skip, repeat)[None],
+            local(gated_gain)[None],
+            jnp.zeros((1, width), jnp.float32),
+        ],
+        0,
+    )
+    state_channel = jnp.concatenate(
+        [
+            conv_kernel[:, ssm_width:],
+            conv_offset[None, ssm_width:],
+            jnp.zeros((3, state_width), jnp.float32),
+        ],
+        0,
+    )
+    local_head = lambda array: lax.dynamic_slice_in_dim(array, rank * heads, heads, 0)
+    head_rows = jnp.pad(
+        jnp.stack([local_head(timestep_bias), -jnp.exp(local_head(decay_log))]),
+        ((0, 6), (0, 128 - heads)),
+    )
+    quarter = HEAD_SIZE // 2
+    frequency = jnp.exp(
+        jnp.arange(quarter, dtype=jnp.float32) * (-2.0 * math.log(ROPE_BASE) / HEAD_SIZE)
+    )
+    angles = jnp.arange(rows, dtype=jnp.float32)[:, None] * frequency[None, :]
+    cosine = jnp.tile(jnp.cos(angles), (1, 4))
+    sinusoid = jnp.sin(angles)
+    sinusoid = jnp.concatenate([-sinusoid, sinusoid, -sinusoid, sinusoid], 1)
+    rank_array = rank.astype(jnp.int32)[None]
+
+    first_weight = place(starts, first_pieces)
+    projected = mm(normed, first_weight)
+    attended, turned, keys, values, logsum = attention_forward(
+        rank_array,
+        projected,
+        (query_at, keyvalue_at, query_width, keyvalue_width),
+        info,
+        label_rows,
+        cosine,
+        sinusoid,
+    )
+    second_weight = place(starts, second_pieces)
+    mamba_weight, attention_weight = second_weight[:, :width], second_weight[:, width:]
+    attention_low = narrow(contract_cols(attended, attention_weight))
+    attention_part = wide(attention_low) + wide(other(attention_low))
+    mixer_widths = (width, state_at, steps_at)
+    gated_low, scanned, square_lanes, dt, cum = mixer_forward(
+        projected, mixer_widths, info, label_rows, channel, state_channel, head_rows
+    )
+    squares = jnp.sum(square_lanes, 1)
+    squares = squares + other(squares)
+    mamba_low = narrow(contract_cols(gated_low, mamba_weight))
+    mamba_part = wide(mamba_low) + wide(other(mamba_low))
+    norm_factor = lax.rsqrt(squares / ssm_width + EPSILON)
+    factor = wide(narrow(norm_factor))[:, None]
+    middle = residual + (factor * mamba_part + attention_part)
+    middle_rms = inverse_rms(middle)
+    hidden_in = narrow(middle * middle_rms * middle_gain)
+    third_weight = place(starts, third_pieces)
+    gateup_full, down_full = third_weight[:, : 2 * hidden], third_weight[:, 2 * hidden :]
+    gateup = mm(hidden_in, gateup_full)
+    gate_part, up_part = gateup[:, :hidden], gateup[:, hidden:]
+    gate_sigmoid = jax.nn.sigmoid(gate_part)
+    activated = narrow(gate_part * gate_sigmoid * up_part)
+
+    grad_activated = mm(cotangent, down_full)
+    grad_gateup = narrow(
+        jnp.concatenate(
+            [
+                grad_activated
+                * up_part
+                * gate_sigmoid
+                * (1.0 + gate_part * (1.0 - gate_sigmoid)),
+                grad_activated * (gate_part * gate_sigmoid),
+            ],
+            1,
+        )
+    )
+    hidden_low = narrow(contract_cols(grad_gateup, gateup_full))
+    grad_hidden = wide(hidden_low) + wide(other(hidden_low))
+    feedforward_low = narrow(contract_cols(activated, down_full))
+    block_output = (
+        own_half(middle)
+        + wide(own_half(feedforward_low))
+        + wide(other(far_half(feedforward_low)))
+    )
+    down_grad = reduce_pieces(narrow(contract_rows(permuted(cotangent), activated)), size)
+    gateup_grad = reduce_pieces(narrow(contract_rows(permuted(hidden_in), grad_gateup)), size)
+    middle_normal = middle * middle_rms
+    middle_gain_part = jnp.sum(grad_hidden * middle_normal, 0)
+    middle_scaled = grad_hidden * middle_gain
+    grad_middle = wide(cotangent) + middle_rms * (
+        middle_scaled - middle_normal * jnp.mean(middle_scaled * middle_normal, -1, keepdims=True)
+    )
+    mix_low = narrow(grad_middle)
+    mix = wide(mix_low)
+    grad_square = narrow(
+        jnp.sum(mix * mamba_part, -1) * -0.5 * norm_factor * norm_factor * norm_factor / ssm_width
+    )
+    grad_mamba = narrow(factor * mix)
+
+    second_grad = reduce_pieces(
+        narrow(
+            jnp.concatenate(
+                [
+                    contract_rows(permuted(grad_mamba), gated_low),
+                    contract_rows(permuted(mix_low), attended),
+                ],
+                1,
+            )
+        ),
+        size,
+    )
+    grad_gated_low = mm(grad_mamba, mamba_weight)
+    lanes = jnp.arange(128, dtype=jnp.int32)[None, :]
+    info = jnp.where(lanes == 5, wide(grad_square)[:, None], info)
+    grad_attended = narrow(mm(mix_low, attention_weight))
+    grad_query, grad_keyvalue = attention_backward(
+        rank_array, grad_attended, turned, keys, values, logsum, info, label_rows, cosine, sinusoid
+    )
+    grad_gate, grad_value, grad_state, grad_steps, channel_grad, state_grad, head_grad = (
+        mixer_backward(
+            projected,
+            mixer_widths,
+            info,
+            label_rows,
+            channel,
+            state_channel,
+            head_rows,
+            scanned,
+            grad_gated_low,
+            dt,
+            cum,
+        )
+    )
+    grad_projected = jnp.concatenate(
+        [grad_gate, grad_value, grad_state, grad_query, grad_keyvalue, grad_steps], 1
+    )
+    normed_partial = contract_cols(grad_projected, first_weight)
+    first_grad = reduce_pieces(
+        narrow(contract_rows(permuted(normed), grad_projected)), size
+    )
+    first_normal = residual * first_rms
+    input_gain_part = jnp.sum(normed_partial * first_normal, 0)
+    normed_low = narrow(normed_partial)
+    normed_grad = wide(own_half(normed_low)) + wide(other(far_half(normed_low)))
+    own_normal = own_half(first_normal)
+    first_scaled = normed_grad * input_gain
+    input_grad = own_half(grad_middle) + own_half(first_rms) * (
+        first_scaled - own_normal * jnp.mean(first_scaled * own_normal, -1, keepdims=True)
+    )
+
+    spread = lambda part, total, start: lax.dynamic_update_slice_in_dim(
+        jnp.zeros(part.shape[:-1] + (total,), jnp.float32), part, start, part.ndim - 1
+    )
+    channel_parts = jnp.concatenate(
+        [spread(channel_grad[:5], ssm_width, rank * width), state_grad[:5]], 1
+    )
+    skip_grad = jnp.sum(channel_grad[5].reshape(heads, repeat), 1)
+    head_parts = spread(
+        jnp.concatenate([head_grad[:2, :heads], skip_grad[None]], 0),
+        timestep_bias.shape[0],
+        rank * heads,
+    )
+    gain_parts = spread(channel_grad[6], ssm_width, rank * width)
+    leader = (rank == 0).astype(jnp.float32)
+    parts = [input_gain_part, middle_gain_part * leader, gain_parts, channel_parts, head_parts]
+    flat = jnp.concatenate([part.reshape(-1) for part in parts])
+    flat = reduce_all(jnp.pad(flat, (0, -flat.shape[0] % 1024)).reshape(-1, 128), size).reshape(-1)
+    summed = []
+    for part in parts:
+        summed.append(flat[: part.size].reshape(part.shape))
+        flat = flat[part.size :]
+    shared = jnp.concatenate(
+        [first_grad[:, state_at:query_at], first_grad[:, keyvalue_at:steps_at]], 1
+    )
+    shared = shared + other(shared)
+    return (
+        block_output,
+        input_grad,
+        summed[0],
+        first_grad[:, :state_at].reshape(shard, 2, width),
+        first_grad[:, steps_at : steps_at + heads],
+        shared[:, :state_width],
+        first_grad[:, query_at:keyvalue_at],
+        shared[:, state_width:],
+        summed[3][:4],
+        summed[3][4],
+        summed[4][0],
+        summed[4][1],
+        summed[4][2],
+        summed[2],
+        second_grad[:, :width].T,
+        second_grad[:, width:].T,
+        summed[1],
+        gateup_grad.reshape(shard, 2, hidden),
+        down_grad.T,
+    )
+
+
 def solution(mesh):
+    fsdp, tp = mesh.shape["fsdp"], mesh.shape["tp"]
+
+    def body(*operands):
+        rows = operands[1].shape[0]
+        if tp == 2 and fsdp % 4 == 0 and rows == 2 * BLOCK:
+            return packed_body(fsdp, *operands)
+        return general_body(*operands)
+
     return jax.shard_map(
         body,
         mesh=mesh,

time: 1320 us -> 440 us (0.33)
  waiting for transfers between devices: 733 us -> 184 us
  blocking collectives: 158 us -> 0 us
  local copies, waits for them, and re-layouts: 165 us -> 50.9 us
  matrix products: 142 us -> 55.9 us
  Pallas kernels: 0 us -> 48.1 us
  starting transfers between devices: 1.52 us -> 48.6 us
  other arithmetic: 82.3 us -> 40.8 us
  between operations: 16.7 us -> 2.86 us
    reduce_scatter x13 -> x0, waiting for transfers between devices: 526 us -> none  [the longest x1 74.3 us: body(): lax.psum_scatter(gateup_wgrad.astype(jnp.bfloat16), 'fsdp', scatter_dimen...]
    ppermute x0 -> x79, waiting for transfers between devices: none -> 184 us  [the longest x12 48.3 us: reduce_pieces(): lax.ppermute(narrow(total), 'fsdp', ring(size))]
    all_gather x8 -> x0, waiting for transfers between devices: 142 us -> none  [the longest x1 48.1 us: body(): lax.all_gather(gateup_weight, 'fsdp', axis=0, tiled=True)]
    all_gather x7 -> x0, blocking collectives: 112 us -> none  [the longest x1 24.6 us: body(): lax.all_gather(state_weight, 'fsdp', axis=0, tiled=True)]
    dot_general x51 -> x5, matrix products: 111 us -> 15.8 us  [mm(): return jnp.dot(left, right, preferred_element_type=jnp.float32)]
    dynamic_update_slice x19 -> x3, local copies, waits for them, and re-layouts: 74 us -> 0.63 us  [packed_body(): lax.dynamic_update_slice_in_dim(jnp.zeros(part.shape[:-1] + (total,), jnp...]
    unnamed x24 -> x0, waiting for transfers between devices: 57 us -> none
    ppermute x0 -> x79, starting transfers between devices: none -> 48.6 us  [the longest x12 13.6 us: gather_pieces(): lax.ppermute(shard, 'fsdp', swaps(size, 2))]
  transfers between devices with their start and end apart: 23 -> 79, of which waited for: 18 -> 30; matrix products, arithmetic and copies ran while one was open for 15% -> 28% of each run, Pallas kernels for 0% -> 10%
where the time goes in v1:
time: 440 us; the launch traced here: 432 us
  waiting for transfers between devices  184 us (42%)
  matrix products  55.9 us (13%)
  local copies, waits for them, and re-layouts  50.9 us (12%)
  starting transfers between devices  48.6 us (11%)
  Pallas kernels  48.1 us (11%)
  other arithmetic  40.8 us (9%)
    ppermute x12, waiting for transfers between devices, reduce_pieces(): lax.ppermute(narrow(total), 'fsdp', ring(size))  48.3 us
    ppermute x4, waiting for transfers between devices, reduce_pieces(): lax.ppermute(own[half:], 'fsdp', swaps(size, 2))  48 us
    ppermute x9, waiting for transfers between devices, gather_pieces(): held.append(lax.ppermute(held[-1], 'fsdp', ring(size)))  44.3 us
    ppermute x9, waiting for transfers between devices, other(): return lax.ppermute(values, 'tp', swaps(2, 1))  29.2 us
    dot_general x5, matrix products, contract_rows(): lax.dot_general(left, right, (((0,), (0,)), ((), ())), preferred_element_...  27.3 us
    unnamed x196, local copies, waits for them, and re-layouts  21.5 us
    pallas_call x1, Pallas kernels, mixer_backward(): pl.pallas_call(mixer_backward_kernel, grid=(pairs,), in_specs=[block_spec...  16.3 us
    dot_general x5, matrix products, mm(): return jnp.dot(left, right, preferred_element_type=jnp.float32)  15.8 us
  transfers between devices with their start and end apart: 79, of which 30 were waited for; matrix products, arithmetic and copies ran while one was open for 28% of the time, Pallas kernels for 10%

profile of v1, /device:TPU:0, one launch (start us, length us, event | category | flops | bytes accessed | tf_op | source)
XLA Modules:
  0.0 431.5 jit_solution(3736161674530876171)
XLA Ops:
  4.9 3.1 collective-permute-start.4
  12.9 4.4 %collective-permute-done.4.refs_5_ = bf16[64,2432]{1,0:T(8,128)(2,1)S(1)} collective-permute-done((bf16[64,2432]{1,0:T(8,128)(2,1)S(1)}, bf16[64,2432]{1,0:T(8,128)(2,1)S(1)}, u32[]{:S(2)}, u32[]{:S(2)}) %collective-permute-start.4) | collective-permute-done | bytes 311328 | tf_op jit(solution)/shard_map/ppermute | solution.py:1232
  19.2 8.4 %collective-permute-done.8.refs_9_ = bf16[64,2432]{1,0:T(8,128)(2,1)S(1)} collective-permute-done((bf16[64,2432]{1,0:T(8,128)(2,1)S(1)}, bf16[64,2432]{1,0:T(8,128)(2,1)S(1)}, u32[]{:S(2)}, u32[]{:S(2)}) %collective-permute-start.8) | collective-permute-done | bytes 311328 | tf_op jit(solution)/shard_map/ppermute | solution.py:1232
  29.1 8.0 %collective-permute-done.12.refs_13_ = bf16[64,2432]{1,0:T(8,128)(2,1)S(1)} collective-permute-done((bf16[64,2432]{1,0:T(8,128)(2,1)S(1)}, bf16[64,2432]{1,0:T(8,128)(2,1)S(1)}, u32[]{:S(2)}, u32[]{:S(2)}) %collective-permute-start.12) | collective-permute-done | bytes 311328 | tf_op jit(solution)/shard_map/ppermute | solution.py:1232
  39.5 4.3 collective-permute-done.20.refs_5_
  56.4 4.5 %collective-permute-done.28.refs_13_ = bf16[64,1024]{1,0:T(8,128)(2,1)} collective-permute-done((bf16[64,1024]{1,0:T(8,128)(2,1)S(1)}, bf16[64,1024]{1,0:T(8,128)(2,1)}, u32[]{:S(2)}, u32[]{:S(2)}) %collective-permute-start.28) | collective-permute-done | bytes 131104 | tf_op jit(solution)/shard_map/ppermute | solution.py:1232
  62.0 4.3 collective-permute-done.22.refs_7_
  68.8 4.8 %place.3 = bf16[1024,2432]{1,0:T(8,128)(2,1)} custom-call(s32[16]{0:T(128)S(1)} %stack.76.refs_0_, bf16[64,2432]{1,0:T(8,128)(2,1)S(1)} %constant_dynamic-update-slice_fusion.refs_1_, bf16[64,2432]{1,0:T(8,128)(2,1)S(1)} %collective-permute-done.1.refs_2_, bf16[64,2432]{1,0:T(8,128)(2,1)S(1)} %collective-permute-done.2.refs_3_, ...), custom_call_target="tpu_custom_call" | custom-call | bytes 9961472 | tf_op jit(solution)/shard_map/place/pallas_call | solution.py:1206
  73.7 7.6 %fusion.49.gate_ref.value_ref.state_ref.steps_ref.query_ref.keyvalue_ref = f32[512,2432]{1,0:T(8,128)} fusion(bf16[1024,2432]{1,0:T(8,128)(2,1)} %place.3, f32[1024]{0:T(1024)S(1)} %copy-done.69, f32[512]{0:T(512)S(1)} %add_rsqrt_fusion.2, bf16[256,1024]{1,0:T(8,128)(2,1)S(1)} %get-tuple-element.138, bf16[256,1024]{1,0:T(8,128)(2,1)S(1)} %get-tuple-element.137), kind=kOutput, calls=%fused_computation.103 | convolution fusion | flops 2553806848 | bytes 11016192 | tf_op jit(solution)/shard_map/dot_general | solution.py:603
  82.4 8.4 %mixer_forward.1 = (bf16[512,768]{1,0:T(8,128)(2,1)S(1)}, f32[512,768]{1,0:T(8,128)S(1)}, f32[512,128]{1,0:T(8,128)S(1)}, f32[512,128]{1,0:T(8,128)S(1)}, f32[512,128]{1,0:T(8,128)S(1)}) custom-call(f32[512,2432]{1,0:T(8,128)} %fusion.49.gate_ref.value_ref.state_ref.steps_ref.query_ref.keyvalue_ref, ...), custom_call_target="tpu_custom_call" | custom-call | flops 4831838208 | bytes 5505024 | tf_op jit(solution)/shard_map/mixer_forward/pallas_call | solution.py:1010
  95.7 4.6 %attention_forward.1 = (bf16[512,256]{1,0:T(8,128)(2,1)S(1)}, bf16[512,256]{1,0:T(8,128)(2,1)S(1)}, bf16[512,128]{1,0:T(8,128)(2,1)S(1)}, bf16[512,128]{1,0:T(8,128)(2,1)S(1)}, f32[512,128]{1,0:T(8,128)S(1)}) custom-call(s32[1]{0:T(128)} %bitcast.25.rank_ref, f32[512,2432]{1,0:T(8,128)} %fusion.49.gate_ref.value_ref.state_ref.steps_ref.query_ref.keyvalue_ref, ...), custom_call_target="tpu_custom_call" | custom-call | flops 1610612736 | bytes 2097152 | tf_op jit(solution)/shard_map/attention_forward/pallas_call | solution.py:1131
  107.1 2.9 place.4
  120.4 4.7 %collective-permute-done.41.refs_9_ = bf16[64,3072]{1,0:T(8,128)(2,1)} collective-permute-done((bf16[64,3072]{1,0:T(8,128)(2,1)}, bf16[64,3072]{1,0:T(8,128)(2,1)}, u32[]{:S(2)}, u32[]{:S(2)}) %collective-permute-start.41) | collective-permute-done | bytes 393248 | tf_op jit(solution)/shard_map/ppermute | solution.py:1232
  127.3 10.0 %collective-permute-done.45.refs_13_ = bf16[64,3072]{1,0:T(8,128)(2,1)} collective-permute-done((bf16[64,3072]{1,0:T(8,128)(2,1)}, bf16[64,3072]{1,0:T(8,128)(2,1)}, u32[]{:S(2)}, u32[]{:S(2)}) %collective-permute-start.45) | collective-permute-done | bytes 393248 | tf_op jit(solution)/shard_map/ppermute | solution.py:1232
  140.4 5.5 %collective-permute-done.43.refs_11_ = bf16[64,3072]{1,0:T(8,128)(2,1)S(1)} collective-permute-done((bf16[64,3072]{1,0:T(8,128)(2,1)}, bf16[64,3072]{1,0:T(8,128)(2,1)S(1)}, u32[]{:S(2)}, u32[]{:S(2)}) %collective-permute-start.43) | collective-permute-done | bytes 393248 | tf_op jit(solution)/shard_map/ppermute | solution.py:1235
  146.5 17.9 %collective-permute-done.32 = bf16[512,1024]{1,0:T(8,128)(2,1)} collective-permute-done((bf16[512,1024]{1,0:T(8,128)(2,1)}, bf16[512,1024]{1,0:T(8,128)(2,1)}, u32[]{:S(2)}, u32[]{:S(2)}) %collective-permute-start.32) | collective-permute-done | bytes 1048608 | tf_op jit(solution)/shard_map/ppermute | solution.py:1306
  164.9 3.1 multiply_reduce_fusion.3
  169.0 6.8 %place.5 = bf16[1024,3072]{1,0:T(8,128)(2,1)} custom-call(s32[16]{0:T(128)S(1)} %copy-done.20, bf16[64,3072]{1,0:T(8,128)(2,1)S(1)} %pad_maximum_fusion.6.refs_1_, bf16[64,3072]{1,0:T(8,128)(2,1)S(1)} %copy-done.1, bf16[64,3072]{1,0:T(8,128)(2,1)} %collective-permute-done.35.refs_3_, bf16[64,3072]{1,0:T(8,128)(2,1)} %collective-permute-done.36.refs_4_, ...), custom_call_target="tpu_custom_call" | custom-call | bytes 12582912 | tf_op jit(solution)/shard_map/place/pallas_call | solution.py:1206
  175.8 4.7 %fusion.7 = f32[512,2048]{1,0:T(8,128)S(1)} fusion(bf16[1024,3072]{1,0:T(8,128)(2,1)} %place.5, f32[512,1024]{1,0:T(8,128)S(1)} %get-tuple-element.128, f32[1024]{0:T(1024)S(1)} %copy-done.68, f32[512]{0:T(512)S(1)} %add_rsqrt_fusion), kind=kOutput, calls=%fused_computation.12 | convolution fusion | flops 2149056512 | bytes 10491904 | tf_op jit(solution)/shard_map/dot_general | solution.py:603
  186.7 3.4 fusion.31
  191.1 7.6 %convolution_convert_fusion.1 = bf16[1024,2048]{1,0:T(8,128)(2,1)} fusion(bf16[512,1024]{1,0:T(8,128)(2,1)} %copy-done.84, bf16[512,1024]{1,0:T(8,128)(2,1)} %copy-done.83, s32[1024]{0:T(1024)S(1)} %fusion.69, f32[512,1024]{1,0:T(8,128)} %copy-done.38, f32[1024]{0:T(1024)S(1)} %copy-done.68, f32[512]{0:T(512)S(1)} %add_rsqrt_fusion), kind=kOutput, calls=%fused_computation.9 | convolution fusion | flops 3230662656 | bytes 8398848 | tf_op jit(solution)/shard_map/dot_general | solution.py:28
  198.7 3.2 slice.366
  201.9 5.6 %convolution_convert_fusion.2 = bf16[1024,1024]{1,0:T(8,128)(2,1)} fusion(bf16[512,1024]{1,0:T(8,128)(2,1)} %copy-done.82, s32[1024]{0:T(1024)S(1)} %fusion.69, bf16[256,1024]{1,0:T(8,128)(2,1)} %copy-done.54, bf16[256,1024]{1,0:T(8,128)(2,1)} %copy-done.52), kind=kOutput, calls=%fused_computation.49 | convolution fusion | flops 2152202240 | bytes 4198400 | tf_op jit(solution)/shard_map/dot_general | solution.py:28
  207.5 2.4 slice.374
  210.4 2.4 convert_add_fusion.7
  212.8 9.5 %collective-permute-done.51 = bf16[512,1024]{1,0:T(8,128)(2,1)} collective-permute-done((bf16[512,1024]{1,0:T(8,128)(2,1)}, bf16[512,1024]{1,0:T(8,128)(2,1)}, u32[]{:S(2)}, u32[]{:S(2)}) %collective-permute-start.51) | collective-permute-done | bytes 1048608 | tf_op jit(solution)/shard_map/ppermute | solution.py:1306
  224.7 4.7 %fusion.9 = (f32[512]{0:T(512)S(1)}, bf16[512,1024]{1,0:T(8,128)(2,1)S(1)}, f32[512,1024]{1,0:T(8,128)}) fusion(bf16[512,1024]{1,0:T(8,128)(2,1)} %collective-permute-done.32, bf16[512,1024]{1,0:T(8,128)(2,1)} %convolution_convert_fusion.4, f32[512]{0:T(512)S(1)} %broadcast_multiply_fusion, f32[512,1024]{1,0:T(8,128)S(1)} %copy-done.39, ...), kind=kLoop, calls=%fused_computation.20 | loop fusion | flops 10485248 | bytes 10496000 | tf_op jit(solution)/shard_map/reduce_sum | solution.py:1477
  232.1 16.3 %mixer_backward.1 = (bf16[512,768]{1,0:T(8,128)(2,1)S(1)}, bf16[512,768]{1,0:T(8,128)(2,1)S(1)}, bf16[512,256]{1,0:T(8,128)(2,1)S(1)}, bf16[512,128]{1,0:T(8,128...) custom-call(f32[512,2432]{1,0:T(8,128)} %fusion.49.gate_ref.value_ref.state_ref.steps_ref.query_ref.key, ...), custom_call_target="tpu_custom_call" | custom-call | flops 14495514624 | bytes 8650752 | tf_op jit(solution)/shard_map/mixer_backward/pallas_call | solution.py:1060
  249.5 4.3 attention_backward.1
  255.5 4.5 %multiply_reduce_fusion.1 = (f32[1024]{0:T(1024)S(1)}, bf16[512,1024]{1,0:T(8,128)(2,1)}, f32[512,1024]{1,0:T(8,128)}) fusion(f32[512]{0:T(512)S(1)} %copy-done.76, bf16[256,1024]{1,0:T(8,128)(2,1)S(1)} %copy-done.49, bf16[256,1024]{1,0:T(8,128)(2,1)S(1)} %copy-done.46, bf16[512,2432]{1,0:T(8,128)(2,1)S(1)} %constant_dynamic-update-slice_fusion.5, ...), kind=kOutput, calls=%fused_computation.35 | convolution fusion | flops 2554330112 | bytes 11671552 | tf_op jit(solution)/shard_map/dot_general | solution.py:34
  260.1 7.9 %convolution_convert_fusion = bf16[1024,2432]{1,0:T(8,128)(2,1)} fusion(bf16[512,2432]{1,0:T(8,128)(2,1)} %copy-done.65, s32[1024]{0:T(1024)S(1)} %fusion.69, f32[1024]{0:T(1024)S(1)} %copy-done.70, f32[512]{0:T(512)S(1)} %copy-done.76, bf16[256,1024]{1,0:T(8,128)(2,1)S(1)} %copy-done.49, bf16[256,1024]{1,0:T(8,128)(2,1)S(1)} %copy-done.46), kind=kOutput, calls=%fused_computation | convolution fusion | flops 3631611904 | bytes 8529920 | tf_op jit(solution)/shard_map/dot_general | solution.py:28
  269.2 3.4 convolution_convert_fusion.3
  273.7 2.8 convolution_convert_fusion.6
  282.4 3.3 slice.336
  289.2 2.4 collective-permute-done.56
  302.0 7.8 %collective-permute-done.75 = bf16[256,1024]{1,0:T(8,128)(2,1)} collective-permute-done((bf16[256,1024]{1,0:T(8,128)(2,1)}, bf16[256,1024]{1,0:T(8,128)(2,1)}, u32[]{:S(2)}, u32[]{:S(2)}) %collective-permute-start.75) | collective-permute-done | bytes 524320 | tf_op jit(solution)/shard_map/ppermute | solution.py:1246
  315.7 5.4 %collective-permute-done.76 = bf16[64,1024]{1,0:T(8,128)(2,1)S(1)} collective-permute-done((bf16[64,1024]{1,0:T(8,128)(2,1)S(1)}, bf16[64,1024]{1,0:T(8,128)(2,1)S(1)}, u32[]{:S(2)}, u32[]{:S(2)}) %collective-permute-start.76) | collective-permute-done | bytes 131104 | tf_op jit(solution)/shard_map/ppermute | solution.py:1251
  321.2 4.3 %collective-permute-done.65 = bf16[256,1024]{0,1:T(8,128)(2,1)S(1)} collective-permute-done((bf16[256,1024]{0,1:T(8,128)(2,1)S(1)}, bf16[256,1024]{0,1:T(8,128)(2,1)S(1)}, u32[]{:S(2)}, u32[]{:S(2)}) %collective-permute-start.65) | collective-permute-done | bytes 524320 | tf_op jit(solution)/shard_map/ppermute | solution.py:1246
  328.6 6.5 %collective-permute-done.66 = bf16[64,1024]{0,1:T(8,128)(2,1)S(1)} collective-permute-done((bf16[64,1024]{0,1:T(8,128)(2,1)S(1)}, bf16[64,1024]{0,1:T(8,128)(2,1)S(1)}, u32[]{:S(2)}, u32[]{:S(2)}) %collective-permute-start.66) | collective-permute-done | bytes 131104 | tf_op jit(solution)/shard_map/ppermute | solution.py:1251
  335.2 2.5 collective-permute-done.78
  338.4 4.9 %collective-permute-done.67 = bf16[64,1024]{0,1:T(8,128)(2,1)S(1)} collective-permute-done((bf16[64,1024]{0,1:T(8,128)(2,1)S(1)}, bf16[64,1024]{0,1:T(8,128)(2,1)S(1)}, u32[]{:S(2)}, u32[]{:S(2)}) %collective-permute-start.67) | collective-permute-done | bytes 131104 | tf_op jit(solution)/shard_map/ppermute | solution.py:1251
  343.7 2.5 add_convert_fusion
  355.9 22.1 %collective-permute-done.59 = bf16[256,2432]{1,0:T(8,128)(2,1)} collective-permute-done((bf16[256,2432]{1,0:T(8,128)(2,1)}, bf16[256,2432]{1,0:T(8,128)(2,1)}, u32[]{:S(2)}, u32[]{:S(2)}) %collective-permute-start.59) | collective-permute-done | bytes 1245216 | tf_op jit(solution)/shard_map/ppermute | solution.py:1246
  381.3 13.9 %collective-permute-done.70 = bf16[256,2048]{1,0:T(8,128)(2,1)} collective-permute-done((bf16[256,2048]{1,0:T(8,128)(2,1)}, bf16[256,2048]{1,0:T(8,128)(2,1)}, u32[]{:S(2)}, u32[]{:S(2)}) %collective-permute-start.70) | collective-permute-done | bytes 1048608 | tf_op jit(solution)/shard_map/ppermute | solution.py:1246
  398.3 8.5 %collective-permute-done.71 = bf16[64,2048]{1,0:T(8,128)(2,1)S(1)} collective-permute-done((bf16[64,2048]{1,0:T(8,128)(2,1)S(1)}, bf16[64,2048]{1,0:T(8,128)(2,1)S(1)}, u32[]{:S(2)}, u32[]{:S(2)}) %collective-permute-start.71) | collective-permute-done | bytes 262176 | tf_op jit(solution)/shard_map/ppermute | solution.py:1251
  407.0 6.5 %collective-permute-done.61 = bf16[64,2432]{1,0:T(8,128)(2,1)S(1)} collective-permute-done((bf16[64,2432]{1,0:T(8,128)(2,1)S(1)}, bf16[64,2432]{1,0:T(8,128)(2,1)S(1)}, u32[]{:S(2)}, u32[]{:S(2)}) %collective-permute-start.61) | collective-permute-done | bytes 311328 | tf_op jit(solution)/shard_map/ppermute | solution.py:1251
  413.6 5.5 %collective-permute-done.72 = bf16[64,2048]{1,0:T(8,128)(2,1)S(1)} collective-permute-done((bf16[64,2048]{1,0:T(8,128)(2,1)S(1)}, bf16[64,2048]{1,0:T(8,128)(2,1)S(1)}, u32[]{:S(2)}, u32[]{:S(2)}) %collective-permute-start.72) | collective-permute-done | bytes 262176 | tf_op jit(solution)/shard_map/ppermute | solution.py:1251
  419.2 4.2 collective-permute-done.62
  (462 shorter events, 132.3 us)
Async XLA Ops:
  4.9 12.5 %collective-permute-start.4 = (bf16[64,2432]{1,0:T(8,128)(2,1)S(1)}, bf16[64,2432]{1,0:T(8,128)(2,1)S(1)}, u32[]{:S(2)}, u32[]{:S(2)}) collective-permute-start(bf16[64,2432]{1,0:T(8,128)(2,1)S(1)} %constant_dynamic-update-slice_fusion.refs_1_), channel_id=1, source_target_pairs={{0,8},{2,10},{4,12},{6,14},{8,16},{10,18},{12,20},{14,22},{16,24},... | collective-permute-start | bytes 933896 | tf_op jit(solution)/shard_map/ppermute | solution.py:1232
  7.9 29.2 %collective-permute-start.1 = (bf16[64,2432]{1,0:T(8,128)(2,1)S(1)}, bf16[64,2432]{1,0:T(8,128)(2,1)S(1)}, u32[]{:S(2)}, u32[]{:S(2)}) collective-permute-start(bf16[64,2432]{1,0:T(8,128)(2,1)S(1)} %constant_dynamic-update-slice_fusion.refs_1_), channel_id=1, source_target_pairs={{0,2},{2,0},{4,6},{6,4},{8,10},{10,8},{12,14},{14,12},{16,18},{18,... | collective-permute-start | bytes 933896 | tf_op jit(solution)/shard_map/ppermute | solution.py:1236
  7.9 21.1 %collective-permute-start.2 = (bf16[64,2432]{1,0:T(8,128)(2,1)S(1)}, bf16[64,2432]{1,0:T(8,128)(2,1)S(1)}, u32[]{:S(2)}, u32[]{:S(2)}) collective-permute-start(bf16[64,2432]{1,0:T(8,128)(2,1)S(1)} %constant_dynamic-update-slice_fusion.refs_1_), channel_id=1, source_target_pairs={{0,4},{2,6},{4,0},{6,2},{8,12},{10,14},{12,8},{14,10},{16,20},{18,... | collective-permute-start | bytes 933896 | tf_op jit(solution)/shard_map/ppermute | solution.py:1235
  9.4 27.8 %collective-permute-start = (bf16[256,1024]{1,0:T(8,128)(2,1)}, bf16[256,1024]{1,0:T(8,128)(2,1)}, u32[]{:S(2)}, u32[]{:S(2)}) collective-permute-start(bf16[256,1024]{1,0:T(8,128)(2,1)} %param.20), channel_id=1, source_target_pairs={{0,1},{1,0},{2,3},{3,2},{4,5},{5,4},{6,7},{7,6},{8,9},{9,8},{10,11... | collective-permute-start | bytes 1572872 | tf_op jit(solution)/shard_map/ppermute | solution.py:1306
  27.7 10.6 %collective-permute-start.6 = (bf16[64,2432]{1,0:T(8,128)(2,1)S(1)}, bf16[64,2432]{1,0:T(8,128)(2,1)}, u32[]{:S(2)}, u32[]{:S(2)}) collective-permute-start(bf16[64,2432]{1,0:T(8,128)(2,1)S(1)} %collective-permute-done.4.refs_5_), channel_id=1, source_target_pairs={{0,4},{2,6},{4,0},{6,2},{8,12},{10,14},{12,8},{14,10},{16,20},{18,... | collective-permute-start | bytes 933896 | tf_op jit(solution)/shard_map/ppermute | solution.py:1235
  37.1 15.1 %collective-permute-start.5 = (bf16[64,2432]{1,0:T(8,128)(2,1)S(1)}, bf16[64,2432]{1,0:T(8,128)(2,1)}, u32[]{:S(2)}, u32[]{:S(2)}) collective-permute-start(bf16[64,2432]{1,0:T(8,128)(2,1)S(1)} %collective-permute-done.4.refs_5_), channel_id=1, source_target_pairs={{0,2},{2,0},{4,6},{6,4},{8,10},{10,8},{12,14},{14,12},{16,18},{18,... | collective-permute-start | bytes 933896 | tf_op jit(solution)/shard_map/ppermute | solution.py:1236
  37.2 15.6 %collective-permute-start.10 = (bf16[64,2432]{1,0:T(8,128)(2,1)S(1)}, bf16[64,2432]{1,0:T(8,128)(2,1)}, u32[]{:S(2)}, u32[]{:S(2)}) collective-permute-start(bf16[64,2432]{1,0:T(8,128)(2,1)S(1)} %collective-permute-done.8.refs_9_), channel_id=1, source_target_pairs={{0,4},{2,6},{4,0},{6,2},{8,12},{10,14},{12,8},{14,10},{16,20},{18,... | collective-permute-start | bytes 933896 | tf_op jit(solution)/shard_map/ppermute | solution.py:1235
  38.3 14.1 %collective-permute-start.7 = (bf16[64,2432]{1,0:T(8,128)(2,1)}, bf16[64,2432]{1,0:T(8,128)(2,1)}, u32[]{:S(2)}, u32[]{:S(2)}) collective-permute-start(bf16[64,2432]{1,0:T(8,128)(2,1)} %collective-permute-done.6.refs_7_), channel_id=1, source_target_pairs={{0,2},{2,0},{4,6},{6,4},{8,10},{10,8},{12,14},{14,12},{16,18},{18,... | collective-permute-start | bytes 933896 | tf_op jit(solution)/shard_map/ppermute | solution.py:1236
  38.4 15.3 %collective-permute-start.14 = (bf16[64,2432]{1,0:T(8,128)(2,1)S(1)}, bf16[64,2432]{1,0:T(8,128)(2,1)}, u32[]{:S(2)}, u32[]{:S(2)}) collective-permute-start(bf16[64,2432]{1,0:T(8,128)(2,1)S(1)} %collective-permute-done.12.refs_13_), channel_id=1, source_target_pairs={{0,4},{2,6},{4,0},{6,2},{8,12},{10,14},{12,8},{14,10},{16,20},{18,... | collective-permute-start | bytes 933896 | tf_op jit(solution)/shard_map/ppermute | solution.py:1235
  52.3 14.5 %collective-permute-start.13 = (bf16[64,2432]{1,0:T(8,128)(2,1)S(1)}, bf16[64,2432]{1,0:T(8,128)(2,1)S(1)}, u32[]{:S(2)}, u32[]{:S(2)}) collective-permute-start(bf16[64,2432]{1,0:T(8,128)(2,1)S(1)} %collective-permute-done.12.refs_13_), channel_id=1, source_target_pairs={{0,2},{2,0},{4,6},{6,4},{8,10},{10,8},{12,14},{14,12},{16,18},{18,... | collective-permute-start | bytes 933896 | tf_op jit(solution)/shard_map/ppermute | solution.py:1236
  52.8 13.5 %collective-permute-start.11 = (bf16[64,2432]{1,0:T(8,128)(2,1)}, bf16[64,2432]{1,0:T(8,128)(2,1)S(1)}, u32[]{:S(2)}, u32[]{:S(2)}) collective-permute-start(bf16[64,2432]{1,0:T(8,128)(2,1)} %collective-permute-done.10.refs_11_), channel_id=1, source_target_pairs={{0,2},{2,0},{4,6},{6,4},{8,10},{10,8},{12,14},{14,12},{16,18},{18,... | collective-permute-start | bytes 933896 | tf_op jit(solution)/shard_map/ppermute | solution.py:1236
  53.7 14.1 %collective-permute-start.15 = (bf16[64,2432]{1,0:T(8,128)(2,1)}, bf16[64,2432]{1,0:T(8,128)(2,1)S(1)}, u32[]{:S(2)}, u32[]{:S(2)}) collective-permute-start(bf16[64,2432]{1,0:T(8,128)(2,1)} %collective-permute-done.14.refs_15_), channel_id=1, source_target_pairs={{0,2},{2,0},{4,6},{6,4},{8,10},{10,8},{12,14},{14,12},{16,18},{18,... | collective-permute-start | bytes 933896 | tf_op jit(solution)/shard_map/ppermute | solution.py:1236
  61.9 19.4 %collective-permute-start.17 = (bf16[64,1024]{1,0:T(8,128)(2,1)S(1)}, bf16[64,1024]{1,0:T(8,128)(2,1)S(1)}, u32[]{:S(2)}, u32[]{:S(2)}) collective-permute-start(bf16[64,1024]{1,0:T(8,128)(2,1)S(1)} %maximum_bitcast_fusion.refs_1_), channel_id=1, source_target_pairs={{0,2},{2,0},{4,6},{6,4},{8,10},{10,8},{12,14},{14,12},{16,18},{18,... | collective-permute-start | bytes 393224 | tf_op jit(solution)/shard_map/ppermute | solution.py:1236
  66.3 28.3 %collective-permute-start.21 = (bf16[64,1024]{1,0:T(8,128)(2,1)S(1)}, bf16[64,1024]{1,0:T(8,128)(2,1)}, u32[]{:S(2)}, u32[]{:S(2)}) collective-permute-start(bf16[64,1024]{1,0:T(8,128)(2,1)S(1)} %collective-permute-done.20.refs_5_), channel_id=1, source_target_pairs={{0,2},{2,0},{4,6},{6,4},{8,10},{10,8},{12,14},{14,12},{16,18},{18,... | collective-permute-start | bytes 393224 | tf_op jit(solution)/shard_map/ppermute | solution.py:1236
  66.3 28.1 %collective-permute-start.19 = (bf16[64,1024]{1,0:T(8,128)(2,1)}, bf16[64,1024]{1,0:T(8,128)(2,1)}, u32[]{:S(2)}, u32[]{:S(2)}) collective-permute-start(bf16[64,1024]{1,0:T(8,128)(2,1)} %collective-permute-done.18.refs_3_), channel_id=1, source_target_pairs={{0,2},{2,0},{4,6},{6,4},{8,10},{10,8},{12,14},{14,12},{16,18},{18,... | collective-permute-start | bytes 393224 | tf_op jit(solution)/shard_map/ppermute | solution.py:1236
  66.8 28.4 %collective-permute-start.26 = (bf16[64,1024]{1,0:T(8,128)(2,1)S(1)}, bf16[64,1024]{1,0:T(8,128)(2,1)}, u32[]{:S(2)}, u32[]{:S(2)}) collective-permute-start(bf16[64,1024]{1,0:T(8,128)(2,1)S(1)} %collective-permute-done.24.refs_9_), channel_id=1, source_target_pairs={{0,4},{2,6},{4,0},{6,2},{8,12},{10,14},{12,8},{14,10},{16,20},{18,... | collective-permute-start | bytes 393224 | tf_op jit(solution)/shard_map/ppermute | solution.py:1235
  67.8 27.0 %collective-permute-start.23 = (bf16[64,1024]{1,0:T(8,128)(2,1)}, bf16[64,1024]{1,0:T(8,128)(2,1)}, u32[]{:S(2)}, u32[]{:S(2)}) collective-permute-start(bf16[64,1024]{1,0:T(8,128)(2,1)} %collective-permute-done.22.refs_7_), channel_id=1, source_target_pairs={{0,2},{2,0},{4,6},{6,4},{8,10},{10,8},{12,14},{14,12},{16,18},{18,... | collective-permute-start | bytes 393224 | tf_op jit(solution)/shard_map/ppermute | solution.py:1236
  81.3 14.1 %collective-permute-start.30 = (bf16[64,1024]{1,0:T(8,128)(2,1)}, bf16[64,1024]{1,0:T(8,128)(2,1)S(1)}, u32[]{:S(2)}, u32[]{:S(2)}) collective-permute-start(bf16[64,1024]{1,0:T(8,128)(2,1)} %collective-permute-done.28.refs_13_), channel_id=1, source_target_pairs={{0,4},{2,6},{4,0},{6,2},{8,12},{10,14},{12,8},{14,10},{16,20},{18,... | collective-permute-start | bytes 393224 | tf_op jit(solution)/shard_map/ppermute | solution.py:1235
  94.6 17.5 %collective-permute-start.37 = (bf16[64,3072]{1,0:T(8,128)(2,1)S(1)}, bf16[64,3072]{1,0:T(8,128)(2,1)}, u32[]{:S(2)}, u32[]{:S(2)}) collective-permute-start(bf16[64,3072]{1,0:T(8,128)(2,1)S(1)} %pad_maximum_fusion.6.refs_1_), channel_id=1, source_target_pairs={{0,8},{2,10},{4,12},{6,14},{8,16},{10,18},{12,20},{14,22},{16,24},... | collective-permute-start | bytes 1179656 | tf_op jit(solution)/shard_map/ppermute | solution.py:1232
  103.0 14.1 %collective-permute-start.50 = (bf16[256,1024]{1,0:T(8,128)(2,1)S(1)}, bf16[256,1024]{1,0:T(8,128)(2,1)S(1)}, u32[]{:S(2)}, u32[]{:S(2)}) collective-permute-start(bf16[256,1024]{1,0:T(8,128)(2,1)S(1)} %copy-done.62), channel_id=1, source_target_pairs={{0,1},{1,0},{2,3},{3,2},{4,5},{5,4},{6,7},{7,6},{8,9},{9,8},{10,11... | collective-permute-start | bytes 1572872 | tf_op jit(solution)/shard_map/ppermute | solution.py:1306
  104.1 15.1 %collective-permute-start.34 = (bf16[64,3072]{1,0:T(8,128)(2,1)S(1)}, bf16[64,3072]{1,0:T(8,128)(2,1)S(1)}, u32[]{:S(2)}, u32[]{:S(2)}) collective-permute-start(bf16[64,3072]{1,0:T(8,128)(2,1)S(1)} %pad_maximum_fusion.6.refs_1_), channel_id=1, source_target_pairs={{0,2},{2,0},{4,6},{6,4},{8,10},{10,8},{12,14},{14,12},{16,18},{18,... | collective-permute-start | bytes 1179656 | tf_op jit(solution)/shard_map/ppermute | solution.py:1236
  104.1 15.1 %collective-permute-start.35 = (bf16[64,3072]{1,0:T(8,128)(2,1)S(1)}, bf16[64,3072]{1,0:T(8,128)(2,1)}, u32[]{:S(2)}, u32[]{:S(2)}) collective-permute-start(bf16[64,3072]{1,0:T(8,128)(2,1)S(1)} %pad_maximum_fusion.6.refs_1_), channel_id=1, source_target_pairs={{0,4},{2,6},{4,0},{6,2},{8,12},{10,14},{12,8},{14,10},{16,20},{18,... | collective-permute-start | bytes 1179656 | tf_op jit(solution)/shard_map/ppermute | solution.py:1235
  105.7 12.5 %collective-permute-start.16 = (f32[512]{0:T(512)}, f32[512]{0:T(512)S(1)}, u32[]{:S(2)}, u32[]{:S(2)}) collective-permute-start(f32[512]{0:T(512)} %reduce_sum.82), channel_id=1, source_target_pairs={{0,1},{1,0},{2,3},{3,2},{4,5},{5,4},{6,7},{7,6},{8,9},{9,8},{10,11... | collective-permute-start | bytes 6152 | tf_op jit(solution)/shard_map/ppermute | solution.py:1306
  112.1 13.0 %collective-permute-start.41 = (bf16[64,3072]{1,0:T(8,128)(2,1)}, bf16[64,3072]{1,0:T(8,128)(2,1)}, u32[]{:S(2)}, u32[]{:S(2)}) collective-permute-start(bf16[64,3072]{1,0:T(8,128)(2,1)} %collective-permute-done.37.refs_5_), channel_id=1, source_target_pairs={{0,8},{2,10},{4,12},{6,14},{8,16},{10,18},{12,20},{14,22},{16,24},... | collective-permute-start | bytes 1179656 | tf_op jit(solution)/shard_map/ppermute | solution.py:1232
  117.1 28.8 %collective-permute-start.33 = (bf16[512,1024]{1,0:T(8,128)(2,1)}, bf16[512,1024]{1,0:T(8,128)(2,1)}, u32[]{:S(2)}, u32[]{:S(2)}) collective-permute-start(bf16[512,1024]{1,0:T(8,128)(2,1)} %convolution_convert_fusion.5), channel_id=1, source_target_pairs={{0,1},{1,0},{2,3},{3,2},{4,5},{5,4},{6,7},{7,6},{8,9},{9,8},{10,11... | collective-permute-start | bytes 3145736 | tf_op jit(solution)/shard_map/ppermute | solution.py:1306
  118.2 46.2 %collective-permute-start.32 = (bf16[512,1024]{1,0:T(8,128)(2,1)}, bf16[512,1024]{1,0:T(8,128)(2,1)}, u32[]{:S(2)}, u32[]{:S(2)}) collective-permute-start(bf16[512,1024]{1,0:T(8,128)(2,1)} %convolution_convert_fusion.4), channel_id=1, source_target_pairs={{0,1},{1,0},{2,3},{3,2},{4,5},{5,4},{6,7},{7,6},{8,9},{9,8},{10,11... | collective-permute-start | bytes 3145736 | tf_op jit(solution)/shard_map/ppermute | solution.py:1306
  125.1 12.1 %collective-permute-start.45 = (bf16[64,3072]{1,0:T(8,128)(2,1)}, bf16[64,3072]{1,0:T(8,128)(2,1)}, u32[]{:S(2)}, u32[]{:S(2)}) collective-permute-start(bf16[64,3072]{1,0:T(8,128)(2,1)} %collective-permute-done.41.refs_9_), channel_id=1, source_target_pairs={{0,8},{2,10},{4,12},{6,14},{8,16},{10,18},{12,20},{14,22},{16,24},... | collective-permute-start | bytes 1179656 | tf_op jit(solution)/shard_map/ppermute | solution.py:1232
  125.2 15.1 %collective-permute-start.39 = (bf16[64,3072]{1,0:T(8,128)(2,1)}, bf16[64,3072]{1,0:T(8,128)(2,1)S(1)}, u32[]{:S(2)}, u32[]{:S(2)}) collective-permute-start(bf16[64,3072]{1,0:T(8,128)(2,1)} %collective-permute-done.37.refs_5_), channel_id=1, source_target_pairs={{0,4},{2,6},{4,0},{6,2},{8,12},{10,14},{12,8},{14,10},{16,20},{18,... | collective-permute-start | bytes 1179656 | tf_op jit(solution)/shard_map/ppermute | solution.py:1235
  126.3 19.7 %collective-permute-start.43 = (bf16[64,3072]{1,0:T(8,128)(2,1)}, bf16[64,3072]{1,0:T(8,128)(2,1)S(1)}, u32[]{:S(2)}, u32[]{:S(2)}) collective-permute-start(bf16[64,3072]{1,0:T(8,128)(2,1)} %collective-permute-done.41.refs_9_), channel_id=1, source_target_pairs={{0,4},{2,6},{4,0},{6,2},{8,12},{10,14},{12,8},{14,10},{16,20},{18,... | collective-permute-start | bytes 1179656 | tf_op jit(solution)/shard_map/ppermute | solution.py:1235
  137.2 27.2 %collective-permute-start.47 = (bf16[64,3072]{1,0:T(8,128)(2,1)}, bf16[64,3072]{1,0:T(8,128)(2,1)S(1)}, u32[]{:S(2)}, u32[]{:S(2)}) collective-permute-start(bf16[64,3072]{1,0:T(8,128)(2,1)} %collective-permute-done.45.refs_13_), channel_id=1, source_target_pairs={{0,4},{2,6},{4,0},{6,2},{8,12},{10,14},{12,8},{14,10},{16,20},{18,... | collective-permute-start | bytes 1179656 | tf_op jit(solution)/shard_map/ppermute | solution.py:1235
  140.3 27.8 %collective-permute-start.42 = (bf16[64,3072]{1,0:T(8,128)(2,1)}, bf16[64,3072]{1,0:T(8,128)(2,1)S(1)}, u32[]{:S(2)}, u32[]{:S(2)}) collective-permute-start(bf16[64,3072]{1,0:T(8,128)(2,1)} %collective-permute-done.41.refs_9_), channel_id=1, source_target_pairs={{0,2},{2,0},{4,6},{6,4},{8,10},{10,8},{12,14},{14,12},{16,18},{18,... | collective-permute-start | bytes 1179656 | tf_op jit(solution)/shard_map/ppermute | solution.py:1236
  145.9 22.1 %collective-permute-start.40 = (bf16[64,3072]{1,0:T(8,128)(2,1)S(1)}, bf16[64,3072]{1,0:T(8,128)(2,1)S(1)}, u32[]{:S(2)}, u32[]{:S(2)}) collective-permute-start(bf16[64,3072]{1,0:T(8,128)(2,1)S(1)} %collective-permute-done.39.refs_7_), channel_id=1, source_target_pairs={{0,2},{2,0},{4,6},{6,4},{8,10},{10,8},{12,14},{14,12},{16,18},{18,... | collective-permute-start | bytes 1179656 | tf_op jit(solution)/shard_map/ppermute | solution.py:1236
  145.9 22.2 %collective-permute-start.46 = (bf16[64,3072]{1,0:T(8,128)(2,1)}, bf16[64,3072]{1,0:T(8,128)(2,1)S(1)}, u32[]{:S(2)}, u32[]{:S(2)}) collective-permute-start(bf16[64,3072]{1,0:T(8,128)(2,1)} %collective-permute-done.45.refs_13_), channel_id=1, source_target_pairs={{0,2},{2,0},{4,6},{6,4},{8,10},{10,8},{12,14},{14,12},{16,18},{18,... | collective-permute-start | bytes 1179656 | tf_op jit(solution)/shard_map/ppermute | solution.py:1236
  185.7 24.7 %collective-permute-start.49 = (bf16[256,1024]{1,0:T(8,128)(2,1)}, bf16[256,1024]{1,0:T(8,128)(2,1)}, u32[]{:S(2)}, u32[]{:S(2)}) collective-permute-start(bf16[256,1024]{1,0:T(8,128)(2,1)} %constant_dynamic-slice_fusion.1), channel_id=1, source_target_pairs={{0,1},{1,0},{2,3},{3,2},{4,5},{5,4},{6,7},{7,6},{8,9},{9,8},{10,11... | collective-permute-start | bytes 1572872 | tf_op jit(solution)/shard_map/ppermute | solution.py:1306
  190.1 32.2 %collective-permute-start.51 = (bf16[512,1024]{1,0:T(8,128)(2,1)}, bf16[512,1024]{1,0:T(8,128)(2,1)}, u32[]{:S(2)}, u32[]{:S(2)}) collective-permute-start(bf16[512,1024]{1,0:T(8,128)(2,1)} %fusion.31), channel_id=1, source_target_pairs={{0,1},{1,0},{2,3},{3,2},{4,5},{5,4},{6,7},{7,6},{8,9},{9,8},{10,11... | collective-permute-start | bytes 3145736 | tf_op jit(solution)/shard_map/ppermute | solution.py:1306
  201.9 146.7 %collective-permute-start.69 = (bf16[512,2048]{1,0:T(8,128)(2,1)}, bf16[512,2048]{1,0:T(8,128)(2,1)}, u32[]{:S(2)}, u32[]{:S(2)}) collective-permute-start(bf16[512,2048]{1,0:T(8,128)(2,1)} %slice.366), channel_id=1, source_target_pairs={{0,2},{2,0},{4,6},{6,4},{8,10},{10,8},{12,14},{14,12},{16,18},{18,... | collective-permute-start | bytes 6291464 | tf_op jit(solution)/shard_map/ppermute | solution.py:1243
  209.9 81.8 %collective-permute-start.74 = (bf16[512,1024]{1,0:T(8,128)(2,1)}, bf16[512,1024]{1,0:T(8,128)(2,1)}, u32[]{:S(2)}, u32[]{:S(2)}) collective-permute-start(bf16[512,1024]{1,0:T(8,128)(2,1)} %slice.374), channel_id=1, source_target_pairs={{0,2},{2,0},{4,6},{6,4},{8,10},{10,8},{12,14},{14,12},{16,18},{18,... | collective-permute-start | bytes 3145736 | tf_op jit(solution)/shard_map/ppermute | solution.py:1243
  281.2 19.1 %collective-permute-start.52 = (bf16[256,1024]{1,0:T(8,128)(2,1)}, bf16[256,1024]{1,0:T(8,128)(2,1)S(1)}, u32[]{:S(2)}, u32[]{:S(2)}) collective-permute-start(bf16[256,1024]{1,0:T(8,128)(2,1)} %constant_dynamic-slice_fusion), channel_id=1, source_target_pairs={{0,1},{1,0},{2,3},{3,2},{4,5},{5,4},{6,7},{7,6},{8,9},{9,8},{10,11... | collective-permute-start | bytes 1572872 | tf_op jit(solution)/shard_map/ppermute | solution.py:1306
  285.8 57.9 %collective-permute-start.58 = (bf16[512,2432]{1,0:T(8,128)(2,1)}, bf16[512,2432]{1,0:T(8,128)(2,1)}, u32[]{:S(2)}, u32[]{:S(2)}) collective-permute-start(bf16[512,2432]{1,0:T(8,128)(2,1)} %slice.336), channel_id=1, source_target_pairs={{0,2},{2,0},{4,6},{6,4},{8,10},{10,8},{12,14},{14,12},{16,18},{18,... | collective-permute-start | bytes 7471112 | tf_op jit(solution)/shard_map/ppermute | solution.py:1243
  291.7 19.4 %collective-permute-start.64 = (bf16[512,1024]{0,1:T(8,128)(2,1)}, bf16[512,1024]{0,1:T(8,128)(2,1)}, u32[]{:S(2)}, u32[]{:S(2)}) collective-permute-start(bf16[512,1024]{0,1:T(8,128)(2,1)} %pad_maximum_fusion.3), channel_id=1, source_target_pairs={{0,2},{2,0},{4,6},{6,4},{8,10},{10,8},{12,14},{14,12},{16,18},{18,... | collective-permute-start | bytes 3145736 | tf_op jit(solution)/shard_map/ppermute | solution.py:1243
  296.0 13.8 %collective-permute-start.75 = (bf16[256,1024]{1,0:T(8,128)(2,1)}, bf16[256,1024]{1,0:T(8,128)(2,1)}, u32[]{:S(2)}, u32[]{:S(2)}) collective-permute-start(bf16[256,1024]{1,0:T(8,128)(2,1)} %slice.376), channel_id=1, source_target_pairs={{0,4},{2,6},{4,0},{6,2},{8,12},{10,14},{12,8},{14,10},{16,20},{18,... | collective-permute-start | bytes 1572872 | tf_op jit(solution)/shard_map/ppermute | solution.py:1246
  312.9 12.6 %collective-permute-start.65 = (bf16[256,1024]{0,1:T(8,128)(2,1)S(1)}, bf16[256,1024]{0,1:T(8,128)(2,1)S(1)}, u32[]{:S(2)}, u32[]{:S(2)}) collective-permute-start(bf16[256,1024]{0,1:T(8,128)(2,1)S(1)} %slice.357), channel_id=1, source_target_pairs={{0,4},{2,6},{4,0},{6,2},{8,12},{10,14},{12,8},{14,10},{16,20},{18,... | collective-permute-start | bytes 1572872 | tf_op jit(solution)/shard_map/ppermute | solution.py:1246
  343.6 10.6 %collective-permute-start.68 = (bf16[64,1024]{0,1:T(8,128)(2,1)S(1)}, bf16[64,1024]{0,1:T(8,128)(2,1)S(1)}, u32[]{:S(2)}, u32[]{:S(2)}) collective-permute-start(bf16[64,1024]{0,1:T(8,128)(2,1)S(1)} %fusion.43), channel_id=1, source_target_pairs={{0,8},{2,10},{4,12},{6,14},{8,16},{10,18},{12,20},{14,22},{16,24},... | collective-permute-start | bytes 393224 | tf_op jit(solution)/shard_map/ppermute | solution.py:1251
  347.3 30.6 %collective-permute-start.59 = (bf16[256,2432]{1,0:T(8,128)(2,1)}, bf16[256,2432]{1,0:T(8,128)(2,1)}, u32[]{:S(2)}, u32[]{:S(2)}) collective-permute-start(bf16[256,2432]{1,0:T(8,128)(2,1)} %slice.338), channel_id=1, source_target_pairs={{0,4},{2,6},{4,0},{6,2},{8,12},{10,14},{12,8},{14,10},{16,20},{18,... | collective-permute-start | bytes 3735560 | tf_op jit(solution)/shard_map/ppermute | solution.py:1246
  353.5 41.6 %collective-permute-start.70 = (bf16[256,2048]{1,0:T(8,128)(2,1)}, bf16[256,2048]{1,0:T(8,128)(2,1)}, u32[]{:S(2)}, u32[]{:S(2)}) collective-permute-start(bf16[256,2048]{1,0:T(8,128)(2,1)} %slice.368), channel_id=1, source_target_pairs={{0,4},{2,6},{4,0},{6,2},{8,12},{10,14},{12,8},{14,10},{16,20},{18,... | collective-permute-start | bytes 3145736 | tf_op jit(solution)/shard_map/ppermute | solution.py:1246
  379.5 18.3 %collective-permute-start.60 = (bf16[64,2432]{1,0:T(8,128)(2,1)S(1)}, bf16[64,2432]{1,0:T(8,128)(2,1)S(1)}, u32[]{:S(2)}, u32[]{:S(2)}) collective-permute-start(bf16[64,2432]{1,0:T(8,128)(2,1)S(1)} %slice.468), channel_id=1, source_target_pairs={{0,8},{2,10},{4,12},{6,14},{8,16},{10,18},{12,20},{14,22},{16,24},... | collective-permute-start | bytes 933896 | tf_op jit(solution)/shard_map/ppermute | solution.py:1251
  397.9 15.5 %collective-permute-start.61 = (bf16[64,2432]{1,0:T(8,128)(2,1)S(1)}, bf16[64,2432]{1,0:T(8,128)(2,1)S(1)}, u32[]{:S(2)}, u32[]{:S(2)}) collective-permute-start(bf16[64,2432]{1,0:T(8,128)(2,1)S(1)} %fusion.38), channel_id=1, source_target_pairs={{0,8},{2,10},{4,12},{6,14},{8,16},{10,18},{12,20},{14,22},{16,24},... | collective-permute-start | bytes 933896 | tf_op jit(solution)/shard_map/ppermute | solution.py:1251
  406.9 12.2 %collective-permute-start.72 = (bf16[64,2048]{1,0:T(8,128)(2,1)S(1)}, bf16[64,2048]{1,0:T(8,128)(2,1)S(1)}, u32[]{:S(2)}, u32[]{:S(2)}) collective-permute-start(bf16[64,2048]{1,0:T(8,128)(2,1)S(1)} %fusion.40), channel_id=1, source_target_pairs={{0,8},{2,10},{4,12},{6,14},{8,16},{10,18},{12,20},{14,22},{16,24},... | collective-permute-start | bytes 786440 | tf_op jit(solution)/shard_map/ppermute | solution.py:1251
  (121 other events, 1402.2 us)
